TPU v7x, 256 devices: a whole 4x4x8 slice. The times are simulated.
256 devices in a mesh: slab: 128 (over z_lo, x, y, core), row: 2 (over z_hi).
Axes of the slice: x: 4, y: 4, z: 8 (z_hi: 2, z_lo: 4; z = z_hi * 4 + z_lo), core: 2. Of those that a mesh axis runs over, the one named last changes fastest.
Arguments:
- start_block: float32 [64, 524288], P(None, ('slab', 'row')), may hold values from -960 to 960
- prior_direction: float32 [64, 524288], P(None, ('slab', 'row')), may hold values from -480 to 480
- col_index: int32 [4096, 3], P(('slab', 'row')), may hold values from 0 to 4095, as said below
- k_blocks: float32 [4096, 3, 128, 128], P(('slab', 'row')), may hold values from -1 to 1
- m_blocks: float32 [4096, 3, 128, 128], P(('slab', 'row')), may hold values from -1 to 1
- k_diagonal: float32 [524288], P(('slab', 'row')), may hold values from 2 to 8
- m_diagonal: float32 [524288], P(('slab', 'row')), may hold values from 1 to 4
Outputs:
- iterate: float32 [64, 524288], P(None, ('slab', 'row'))
- prior: float32 [64, 524288], P(None, ('slab', 'row'))
Inputs may be any that keep to these rules, and one draw needn't show every extreme that they name: col_index[g, 0] = g; entries 1 and 2 of row g are block rows other than g within 2 of g (they may be equal); col_index[g, j] = h for j >= 1 exactly when col_index[h, j] = g.
All inputs are finite; a program needn't handle non-finite values.
Results may differ from a plain program's by a relative error of at most 0.0003.
Values sent between devices are 32-bit elements; how exact they have to be, the bound alone decides.
No kernel may reach another device: no remote copies, remote signals or barrier semaphores. Data moves between devices by JAX's collectives and lax.ppermute only.
A program may use at most 64 MiB of HBM per device.

v0:
```python
import jax
import jax.numpy as jnp
from jax import lax
from jax.experimental import pallas as pl
from jax.experimental.pallas import tpu as pltpu
from jax.sharding import PartitionSpec as P

COLS = 64
BS = 128
FACE = 2
NNZ = 3
AXES = ("slab", "row")
HIGHEST = lax.Precision.HIGHEST
STEP = 2
QUARTER = 160
VMEM_LIMIT = 48 * 1024 * 1024


def coords(i):
    zh, c, y, x, zl = i & 1, (i >> 1) & 1, (i >> 2) & 3, (i >> 4) & 3, (i >> 6) & 3
    return {"x": x, "y": y, "z": zh * 4 + zl, "c": c}


def flat(d):
    zh, zl = d["z"] >> 2, d["z"] & 3
    return (((zl * 4 + d["x"]) * 4 + d["y"]) * 2 + d["c"]) * 2 + zh


def partner(x, axis, k):
    pairs = []
    for i in range(256):
        d = coords(i)
        d[axis] ^= k
        pairs.append((i, flat(d)))
    return lax.ppermute(x, AXES, pairs)


ROUNDS = (("c", (1,)), ("x", (1, 2, 3)), ("y", (1, 2, 3)), ("z", (1, 2, 3)), ("z", (4,)))


def all_sum(x, given=None, tasks=None):
    for n, (axis, ks) in enumerate(ROUNDS):
        task = (tasks or {}).get(n)
        if task is not None:
            x, given = lax.optimization_barrier((x, given))
            given = task(*given)
        for part in [partner(x, axis, k) for k in ks]:
            x = x + part
        if task is not None:
            x, given = lax.optimization_barrier((x, given))
    return (x, given) if tasks else x


def x_coord():
    return (lax.axis_index("slab") >> 3) & 3


def all_sum_quarters(quarters):
    own = quarters[0]
    for part in [partner(quarters[k], "x", k) for k in (1, 2, 3)]:
        own = own + part
    for axis, ks in ROUNDS:
        if axis != "x":
            for part in [partner(own, axis, k) for k in ks]:
                own = own + part
    return [own] + [partner(own, "x", k) for k in (1, 2, 3)]


def exchange(edges):
    head, tail = edges
    count = lax.axis_size("slab") * lax.axis_size("row")
    low = lax.ppermute(tail, AXES, [(i, i + 1) for i in range(count - 1)])
    return low, lax.ppermute(head, AXES, [(i + 1, i) for i in range(count - 1)])


def split(x):
    hi = x.astype(jnp.bfloat16)
    return hi, (x - hi.astype(jnp.float32)).astype(jnp.bfloat16)


def dot3(a, b, dims):
    def dot(u, v):
        return lax.dot_general(u, v, (dims, ((), ())), preferred_element_type=jnp.float32)

    return dot(a[0], b[0]) + (dot(a[0], b[1]) + dot(a[1], b[0]))


NT = ((1,), (1,))
TN = ((0,), (0,))
NN = ((1,), (0,))


def exact(a, b, dims=NN):
    return lax.dot_general(a, b, (dims, ((), ())), precision=HIGHEST, preferred_element_type=jnp.float32)


def sym(a):
    return 0.5 * (a + a.T)


def factor_inverses(mats):
    rows = lax.broadcasted_iota(jnp.int32, (COLS, 1), 0)
    eye = (
        lax.broadcasted_iota(jnp.int32, (COLS, COLS), 0) == lax.broadcasted_iota(jnp.int32, (COLS, COLS), 1)
    ).astype(jnp.float32)
    work = [jnp.concatenate([a, eye], 1) for a in mats]
    for j in range(0, COLS, 2):
        for n, w in enumerate(work):
            r1, r2 = w[j : j + 1, :], w[j + 1 : j + 2, :]
            a, b, c = r1[:, j : j + 1], r1[:, j + 1 : j + 2], r2[:, j + 1 : j + 2]
            scale = 1.0 / (a * c - b * b)
            u1, u2 = (c * r1 - b * r2) * scale, (a * r2 - b * r1) * scale
            below = w[:, j : j + 1] * u1 + w[:, j + 1 : j + 2] * u2
            work[n] = w - jnp.where(rows > j + 1, below, jnp.where(rows == j + 1, (b / a) * r1, 0.0))
    out = []
    for w in work:
        d = jnp.sum(w[:, :COLS] * eye, axis=1, keepdims=True)
        r = lax.rsqrt(d)
        r = r * (1.5 - 0.5 * d * r * r)
        out.append(w[:, COLS:] * r)
    return out


def first_parts(first):
    return (
        (sym(first[0:64, 0:64]), first[64:128, 0:64], sym(first[128:192, 0:64])),
        (sym(first[0:64, 64:128]), first[64:128, 64:128], sym(first[128:192, 64:128])),
    )


def halves(first, second):
    out = []
    for n, (xx, px, pp) in enumerate(first_parts(first)):
        sx, sp = second[64 * n : 64 * n + 64, 0:64], second[64 * n : 64 * n + 64, 64:128]
        ss = sym(second[128:192, 64 * n : 64 * n + 64])
        out.append(
            jnp.concatenate(
                [
                    jnp.concatenate([xx, px.T, sx.T], 1),
                    jnp.concatenate([px, pp, sp.T], 1),
                    jnp.concatenate([sx, sp, ss], 1),
                ],
                0,
            )
        )
    return out


def prepare(first, l1, out_ref):
    (_, px_k, pp_k), (xx_m, px_m, _) = first_parts(first)
    y1 = exact(l1, xx_m)
    l21 = exact(px_k, l1, NT)
    (l2,) = factor_inverses([pp_k - exact(l21, l21, NT)])
    y2 = exact(l2, px_m - exact(l21, y1))
    for n, part in enumerate((l1, l2, l21, y1, y2)):
        out_ref[64 * n : 64 * n + 64] = part


def chain(first, second, ready, total_rows):
    l1, l2, l21, y1, y2 = (ready[64 * n : 64 * n + 64] for n in range(5))
    gram_k, gram_m = halves(first, second)
    sx_k, sp_k, ss_k, sx_m = gram_k[128:, 0:64], gram_k[128:, 64:128], gram_k[128:, 128:], gram_m[128:, 0:64]
    l31 = exact(sx_k, l1, NT)
    l32 = exact(sp_k - exact(l31, l21, NT), l2, NT)
    (l3,) = factor_inverses([ss_k - exact(l31, l31, NT) - exact(l32, l32, NT)])
    z3 = exact(l3, exact(l3, sx_m - exact(l31, y1) - exact(l32, y2)), TN)
    z2 = exact(l2, y2 - exact(l32, z3, TN), TN)
    z1 = exact(l1, y1 - exact(l21, z2, TN) - exact(l31, z3, TN), TN)
    coeffs = jnp.concatenate([z1, z2, z3], 0)
    norm = sym(exact(coeffs, exact(gram_m, coeffs), TN))
    (ln,) = factor_inverses([norm * (1.0 / total_rows)])
    return exact(coeffs, ln, NT), gram_k, gram_m


def both(mixing):
    return jnp.concatenate([mixing, jnp.concatenate([jnp.zeros((64, 64), jnp.float32), mixing[64:]], 0)], 1)


def block_row(t, g, col_ref, k_ref, m_ref, hi_ref, lo_ref):
    acc = None
    for j in range(NNZ):
        at = col_ref[g, j]
        w = split(jnp.concatenate([k_ref[t, j], m_ref[t, j]], 0))
        term = dot3((hi_ref[at], lo_ref[at]), w, NT)
        acc = term if acc is None else acc + term
    return acc


def fill(hi_ref, lo_ref, at, tiles):
    for b in range(tiles.shape[1] // BS):
        hi_ref[at + b], lo_ref[at + b] = split(tiles[:, b * BS : (b + 1) * BS])


def pair_steps(first, col_ref, xp_ref, k_ref, m_ref, kd_ref, md_ref, out, hi_ref, lo_ref, acc_ref):
    kv_ref, mv_ref, parts_ref = out
    for t in range(STEP):
        g = first + t
        at = slice(t * BS, (t + 1) * BS)
        acc = block_row(t, g, col_ref, k_ref, m_ref, hi_ref, lo_ref)
        tile = xp_ref[:, pl.ds(pl.multiple_of(g * BS, BS), BS)]
        kv = acc[:, :BS] + kd_ref[:, at] * tile
        mv = acc[:, BS:] + md_ref[:, at] * tile
        kv_ref[:, at] = kv
        mv_ref[:, at] = mv
        parts_ref[:, at] = jnp.concatenate([kv[0:64], mv[0:64]], 0) / kd_ref[:, at]
        acc_ref[...] += dot3(split(jnp.concatenate([kv, mv], 0)), (hi_ref[g + FACE], lo_ref[g + FACE]), NT)


def pair_inner(col_ref, xp_ref, k_ref, m_ref, kd_ref, md_ref, kv_ref, mv_ref, parts_ref, acc_ref, hi_ref, lo_ref):
    i = pl.program_id(0)

    @pl.when(i == 0)
    def _():
        acc_ref[...] = jnp.zeros_like(acc_ref)
        fill(hi_ref, lo_ref, FACE, xp_ref[...])

    out = (kv_ref, mv_ref, parts_ref)
    pair_steps(i * STEP + FACE, col_ref, xp_ref, k_ref, m_ref, kd_ref, md_ref, out, hi_ref, lo_ref, acc_ref)


def fill_edges(v_ref, low_ref, high_ref, hi_ref, lo_ref):
    rows = v_ref.shape[1]
    blocks = rows // BS
    fill(hi_ref, lo_ref, 0, low_ref[...])
    fill(hi_ref, lo_ref, FACE, v_ref[:, : 2 * FACE * BS])
    fill(hi_ref, lo_ref, blocks - FACE, v_ref[:, rows - 2 * FACE * BS :])
    fill(hi_ref, lo_ref, FACE + blocks, high_ref[...])
    return blocks


def pair_edges(
    col_ref, xp_ref, low_ref, high_ref, part_ref, kvin_ref, mvin_ref, partsin_ref, k_ref, m_ref, kd_ref, md_ref,
    kv_ref, mv_ref, parts_ref, gram_ref, hi_ref, lo_ref, acc_ref,
):
    i = pl.program_id(0)

    @pl.when(i == 0)
    def _():
        acc_ref[...] = part_ref[...]
        fill_edges(xp_ref, low_ref, high_ref, hi_ref, lo_ref)

    first = i * (xp_ref.shape[1] // BS - FACE)
    out = (kv_ref, mv_ref, parts_ref)
    pair_steps(first, col_ref, xp_ref, k_ref, m_ref, kd_ref, md_ref, out, hi_ref, lo_ref, acc_ref)

    @pl.when(i == pl.num_programs(0) - 1)
    def _():
        gram = acc_ref[...]
        gram_ref[0:64] = jnp.concatenate([gram[0:64, 0:64], gram[128:192, 0:64]], 1)
        gram_ref[64:128] = jnp.concatenate([gram[64:128, 0:64], gram[192:256, 0:64]], 1)
        gram_ref[128:192] = jnp.concatenate([gram[64:128, 64:128], gram[192:256, 64:128]], 1)


def parts_steps(first, col_ref, xp_ref, parts_ref, k_ref, m_ref, kd_ref, md_ref, kv_ref, mv_ref, hi_ref, lo_ref, acc_ref):
    for t in range(STEP):
        g = first + t
        at = slice(t * BS, (t + 1) * BS)
        here = pl.ds(pl.multiple_of(g * BS, BS), BS)
        acc = block_row(t, g, col_ref, k_ref, m_ref, hi_ref, lo_ref)
        tile = parts_ref[:, here]
        kv = acc[:, :BS] + kd_ref[:, at] * tile
        mv = acc[:, BS:] + md_ref[:, at] * tile
        kv_ref[:, at] = kv
        mv_ref[:, at] = mv
        basis = tuple(jnp.concatenate([u, v[g + FACE]], 0) for u, v in zip(split(xp_ref[:, here]), (hi_ref, lo_ref)))
        acc_ref[...] += dot3(split(jnp.concatenate([kv, mv], 0)), basis, NT)


def parts_inner(col_ref, xp_ref, parts_ref, k_ref, m_ref, kd_ref, md_ref, kv_ref, mv_ref, acc_ref, hi_ref, lo_ref):
    i = pl.program_id(0)

    @pl.when(i == 0)
    def _():
        acc_ref[...] = jnp.zeros_like(acc_ref)
        fill(hi_ref, lo_ref, FACE, parts_ref[...])

    parts_steps(
        i * STEP + FACE, col_ref, xp_ref, parts_ref, k_ref, m_ref, kd_ref, md_ref, kv_ref, mv_ref, hi_ref, lo_ref, acc_ref
    )


def parts_edges(
    col_ref, at_ref, xp_ref, parts_ref, low_ref, high_ref, part_ref, gram_ref, kvin_ref, mvin_ref, k_ref, m_ref, kd_ref, md_ref,
    kv_ref, mv_ref, q0_ref, q1_ref, q2_ref, q3_ref, hi_ref, lo_ref, acc_ref, all_ref,
):
    i = pl.program_id(0)

    @pl.when(i == 0)
    def _():
        acc_ref[...] = part_ref[...]
        fill_edges(parts_ref, low_ref, high_ref, hi_ref, lo_ref)

    first = i * (xp_ref.shape[1] // BS - FACE)
    parts_steps(
        first, col_ref, xp_ref, parts_ref, k_ref, m_ref, kd_ref, md_ref, kv_ref, mv_ref, hi_ref, lo_ref, acc_ref
    )

    @pl.when(i == pl.num_programs(0) - 1)
    def _():
        gram = acc_ref[...]
        all_ref[0:192] = gram_ref[...]
        all_ref[192:448] = gram[:, 0:128]
        all_ref[448:512] = jnp.concatenate([gram[0:64, 128:192], gram[128:192, 128:192]], 1)
        all_ref[512:576] = jnp.concatenate([gram[64:128, 128:192], gram[192:256, 128:192]], 1)
        all_ref[576:640] = jnp.concatenate([gram[64:128, 192:256], gram[192:256, 192:256]], 1)
        for k, out in enumerate((q0_ref, q1_ref, q2_ref, q3_ref)):
            out[...] = all_ref[pl.ds(pl.multiple_of((at_ref[0] ^ k) * QUARTER, 8), QUARTER), :]


def search_steps(first, col_ref, xp_ref, s_ref, k_ref, m_ref, kd_ref, md_ref, hi_ref, lo_ref, acc_ref):
    for t in range(STEP):
        g = first + t
        at = slice(t * BS, (t + 1) * BS)
        here = pl.ds(pl.multiple_of(g * BS, BS), BS)
        acc = block_row(t, g, col_ref, k_ref, m_ref, hi_ref, lo_ref)
        s = s_ref[:, here]
        ks = acc[:, :BS] + kd_ref[:, at] * s
        ms = acc[:, BS:] + md_ref[:, at] * s
        basis = tuple(jnp.concatenate([u, v[g + FACE]], 0) for u, v in zip(split(xp_ref[:, here]), (hi_ref, lo_ref)))
        acc_ref[...] += dot3(split(jnp.concatenate([ks, ms], 0)), basis, NT)


def search_inner(col_ref, xp_ref, s_ref, k_ref, m_ref, kd_ref, md_ref, acc_ref, hi_ref, lo_ref):
    i = pl.program_id(0)

    @pl.when(i == 0)
    def _():
        acc_ref[...] = jnp.zeros_like(acc_ref)
        fill(hi_ref, lo_ref, FACE, s_ref[...])

    search_steps(i * STEP + FACE, col_ref, xp_ref, s_ref, k_ref, m_ref, kd_ref, md_ref, hi_ref, lo_ref, acc_ref)


def search_edges(col_ref, xp_ref, s_ref, low_ref, high_ref, part_ref, k_ref, m_ref, kd_ref, md_ref, gram_ref, hi_ref, lo_ref, acc_ref):
    i = pl.program_id(0)

    @pl.when(i == 0)
    def _():
        acc_ref[...] = part_ref[...]
        fill_edges(s_ref, low_ref, high_ref, hi_ref, lo_ref)

    first = i * (s_ref.shape[1] // BS - FACE)
    search_steps(first, col_ref, xp_ref, s_ref, k_ref, m_ref, kd_ref, md_ref, hi_ref, lo_ref, acc_ref)

    @pl.when(i == pl.num_programs(0) - 1)
    def _():
        gram = acc_ref[...]
        gram_ref[0:128] = gram[:, 0:128]
        gram_ref[128:192] = jnp.concatenate([gram[0:64, 128:192], gram[64:128, 128:192]], 1)


def factor_pair(first_ref, inv_ref, ready_ref):
    prepare(first_ref[...], inv_ref[...], ready_ref)


def next_first(first_ref, second_ref, pair_ref, firsto_ref, inv_ref):
    pair = pair_ref[...]
    gram_k, gram_m = halves(first_ref[...], second_ref[...])
    next_k = exact(pair, exact(gram_k, pair), TN)
    next_m = exact(pair, exact(gram_m, pair), TN)
    firsto_ref[0:64] = jnp.concatenate([next_k[0:64, 0:64], next_m[0:64, 0:64]], 1)
    firsto_ref[64:128] = jnp.concatenate([next_k[64:128, 0:64], next_m[64:128, 0:64]], 1)
    firsto_ref[128:192] = jnp.concatenate([next_k[64:128, 64:128], next_m[64:128, 64:128]], 1)
    (inv,) = factor_inverses([sym(next_k[0:64, 0:64])])
    inv_ref[...] = inv


def search_gram(both_parts, ritz):
    one = jnp.concatenate([both_parts[192:256], both_parts[320:384]], 1)
    two = jnp.concatenate([both_parts[256:320], both_parts[384:448]], 1)
    crossed = jnp.concatenate([both_parts[512:576], both_parts[576:640]], 1)
    old = one - exact(ritz, two, TN)
    crossed = exact(ritz, crossed, TN)
    own = []
    for n in range(2):
        at = slice(64 * n, 64 * n + 64)
        mixed = crossed[:, at]
        own.append(sym(both_parts[448:512, at]) - mixed - mixed.T + exact(crossed[:, 128 + 64 * n : 192 + 64 * n], ritz))
    return jnp.concatenate([old[:, 0:128], old[:, 128:256], jnp.concatenate(own, 1)], 0)


def second_search(
    total_rows, at_ref, q0_ref, q1_ref, q2_ref, q3_ref, kv_ref, mv_ref, ks_ref, ms_ref, kd_ref,
    s_ref, pair_ref, spread_ref, first_ref, second_ref, all_ref, ready_ref,
):
    for k, quarter in enumerate((q0_ref, q1_ref, q2_ref, q3_ref)):
        all_ref[pl.ds(pl.multiple_of((at_ref[0] ^ k) * QUARTER, 8), QUARTER), :] = quarter[...]
    first = all_ref[0:192]
    first_ref[...] = first
    (xx_k, _, _), (xx_m, _, _) = first_parts(first)
    inv, inv_k = factor_inverses([xx_m, xx_k])
    ritz = exact(inv, exact(inv, xx_k), TN)
    prepare(first, inv_k, ready_ref)
    second = search_gram(all_ref[...], ritz)
    second_ref[...] = second
    mixing, gram_k, _ = chain(first, second, ready_ref[...], total_rows)
    pair = both(mixing)
    pair_ref[...] = pair
    spread = jnp.concatenate([pair, -exact(ritz, pair[128:192])], 0)
    spread_ref[...] = spread
    new_ritz = sym(exact(mixing, exact(gram_k, mixing), TN)) * (1.0 / total_rows)
    weights = split(jnp.concatenate([spread[:, 0:64], -exact(spread[:, 0:64], new_ritz)], 0))
    for b in range(0, s_ref.shape[1], 512):
        at = slice(b, b + 512)
        parts = split(jnp.concatenate([kv_ref[:, at], ks_ref[:, at], mv_ref[:, at], ms_ref[:, at]], 0))
        s_ref[:, at] = dot3(weights, parts, TN) / kd_ref[:, at]


def mix(pair, xp_ref, s_ref, at):
    return dot3(pair, split(jnp.concatenate([xp_ref[:, at], s_ref[:, at]], 0)), TN)


def mix_pair(pair_ref, xp_ref, s_ref, xpo_ref):
    pair = split(pair_ref[...])
    for b in range(0, s_ref.shape[1], 512):
        at = slice(b, b + 512)
        xpo_ref[:, at] = mix(pair, xp_ref, s_ref, at)


def last_kernel(total_rows, first_ref, second_ref, ready_ref, xp_ref, s_ref, xo_ref, po_ref):
    mixing, _, _ = chain(first_ref[...], second_ref[...], ready_ref[...], total_rows)
    pair = split(both(mixing))
    for b in range(0, s_ref.shape[1], 512):
        at = slice(b, b + 512)
        new = mix(pair, xp_ref, s_ref, at)
        xo_ref[:, at] = new[0:64]
        po_ref[:, at] = new[64:128]


def whole():
    return pl.BlockSpec(memory_space=pltpu.VMEM)


def smem():
    return pl.BlockSpec(memory_space=pltpu.SMEM)


def anywhere():
    return pl.BlockSpec(memory_space=pl.ANY)


def f32(*shape):
    return jax.ShapeDtypeStruct(shape, jnp.float32)


def bf16_blocks(extended, rows):
    return [pltpu.VMEM((extended, rows, BS), jnp.bfloat16)] * 2


def call(kernel, name, ins, outs, shapes, scratch=(), grid=None, aliases=None, flops=0, moved=0):
    kwargs = {} if grid is None else {"grid": grid}
    return pl.pallas_call(
        kernel,
        in_specs=ins,
        out_specs=outs,
        out_shape=shapes,
        scratch_shapes=list(scratch),
        input_output_aliases=aliases or {},
        compiler_params=pltpu.CompilerParams(vmem_limit_bytes=VMEM_LIMIT),
        cost_estimate=pl.CostEstimate(flops=flops, bytes_accessed=moved, transcendentals=0),
        name=name,
        **kwargs,
    )


def shards(start_block, prior_direction, col_index, k_blocks, m_blocks, k_diagonal, m_diagonal):
    blocks = col_index.shape[0]
    rows = start_block.shape[1]
    devices = lax.axis_size("slab") * lax.axis_size("row")
    total_rows = float(rows * devices)
    edge = FACE * BS
    first_block = (lax.axis_index("slab") * lax.axis_size("row") + lax.axis_index("row")) * blocks - FACE
    col = col_index - first_block
    kd, md = k_diagonal[None, :], m_diagonal[None, :]
    inner, outer = ((blocks - 2 * FACE) // STEP,), (2,)
    last = blocks // STEP - 1
    extended = blocks + 2 * FACE

    def stored(at):
        blocked = pl.BlockSpec((STEP, NNZ, BS, BS), lambda i: (at(i), 0, 0, 0))
        return [blocked] * 2 + columns(1, at)

    def columns(height, at, count=2):
        return [pl.BlockSpec((height, STEP * BS), lambda i: (0, at(i)))] * count

    def inside(i):
        return i + 1

    def at_edge(i):
        return i * last

    def edges(v):
        return v[:, :edge], v[:, rows - edge :]

    big = {"flops": 3 * 2 * 2 * 128 * 384 * 256 * blocks, "moved": 8 * blocks * NNZ * BS * BS}
    matrices = (k_blocks, m_blocks, kd, md)

    xp = jnp.concatenate([start_block, prior_direction], 0)
    low, high = exchange(edges(xp))
    kv, mv, parts, part = call(
        pair_inner, "pair_inner",
        [smem(), whole()] + stored(inside),
        columns(128, inside, 3) + [whole()],
        [f32(128, rows)] * 3 + [f32(256, 128)],
        bf16_blocks(extended, 128), inner, **big,
    )(col, xp, *matrices)
    kv, mv, parts, gram = call(
        pair_edges, "pair_edges",
        [smem()] + [whole()] * 4 + [anywhere()] * 3 + stored(at_edge),
        columns(128, at_edge, 3) + [whole()],
        [f32(128, rows)] * 3 + [f32(192, 128)],
        bf16_blocks(extended, 128) + [pltpu.VMEM((256, 128), jnp.float32)], outer, {5: 0, 6: 1, 7: 2},
    )(col, xp, low, high, part, kv, mv, parts, *matrices)

    low, high = exchange(edges(parts))
    ks, ms, part = call(
        parts_inner, "parts_inner",
        [smem()] + [whole()] * 2 + stored(inside),
        columns(128, inside) + [whole()],
        [f32(128, rows), f32(128, rows), f32(256, 256)],
        bf16_blocks(extended, 128), inner, **big,
    )(col, xp, parts, *matrices)
    at = x_coord().astype(jnp.int32)[None]
    ks, ms, *quarters = call(
        parts_edges, "parts_edges",
        [smem()] * 2 + [whole()] * 6 + [anywhere()] * 2 + stored(at_edge),
        columns(128, at_edge) + [whole()] * 4,
        [f32(128, rows), f32(128, rows)] + [f32(QUARTER, 128)] * 4,
        bf16_blocks(extended, 128) + [pltpu.VMEM((256, 256), jnp.float32), pltpu.VMEM((4 * QUARTER, 128), jnp.float32)],
        outer, {8: 0, 9: 1},
    )(col, at, xp, parts, low, high, part, gram, ks, ms, *matrices)

    quarters = all_sum_quarters(quarters)

    new, pair, spread, first, second = call(
        lambda *refs: second_search(total_rows, *refs), "second_search",
        [smem()] + [whole()] * 9, [whole()] * 5,
        [f32(64, rows), f32(192, 128), f32(256, 128), f32(192, 128), f32(192, 128)],
        [pltpu.VMEM((4 * QUARTER, 128), jnp.float32), pltpu.VMEM((320, 64), jnp.float32)],
    )(at, *quarters, kv, mv, ks, ms, kd)

    def factor(first, inv):
        return first, call(factor_pair, "factor_pair", [whole()] * 2, whole(), f32(320, 64))(first, inv)

    def grams(first, second, pair):
        return call(
            next_first, "next_first", [whole()] * 3, [whole()] * 2, [f32(192, 128), f32(64, 64)]
        )(first, second, pair)

    low, high = exchange(edges(new))
    xp = call(mix_pair, "mix_pair", [whole()] * 3, whole(), f32(128, rows))(spread, xp, parts)
    (part,) = call(
        search_inner, "second_inner",
        [smem()] + [whole()] * 2 + stored(inside), [whole()], [f32(128, 192)],
        bf16_blocks(extended, 64), inner, **big,
    )(col, xp, new, *matrices)
    (gram,) = call(
        search_edges, "second_edges",
        [smem()] + [whole()] * 5 + stored(at_edge), [whole()], [f32(192, 128)],
        bf16_blocks(extended, 64) + [pltpu.VMEM((128, 192), jnp.float32)], outer,
    )(col, xp, new, low, high, part, *matrices)

    second, (first, ready) = all_sum(gram, (first, second, pair), {3: grams, 4: factor})

    iterate, prior = call(
        lambda *refs: last_kernel(total_rows, *refs), "last_mix",
        [whole()] * 5, [whole()] * 2, [f32(64, rows)] * 2,
    )(first, second, ready, xp, new)
    return (iterate, prior)


def solution(mesh):
    in_specs = (
        P(None, ("slab", "row")),
        P(None, ("slab", "row")),
        P(("slab", "row"), None),
        P(("slab", "row"), None, None, None),
        P(("slab", "row"), None, None, None),
        P(("slab", "row")),
        P(("slab", "row")),
    )
    out_specs = (P(None, ("slab", "row")), P(None, ("slab", "row")))
    return jax.shard_map(shards, mesh=mesh, in_specs=in_specs, out_specs=out_specs, check_vma=False)
```

profile of v0, /device:TPU:2, one launch (start us, length us, event | category | flops | bytes accessed | tf_op | source)
XLA Modules:
  0.0 206.7 jit_solution(4506258531787739358)
XLA Ops:
  0.6 1.1 constant_dynamic-update-slice_fusion.1
  1.7 1.1 constant_dynamic-update-slice_fusion.xp_ref
  2.8 11.0 %collective-permute-start.1 = (f32[128,256]{1,0:T(8,128)S(1)}, f32[128,256]{1,0:T(8,128)S(1)}, u32[]{:S(2)}, u32[]{:S(2)}) collective-permute-start(f32[128,256]{1,0:T(8,128)S(1)} %get-tuple-element.72), channel_id=1, source_target_pairs={{1,0},{2,1},{3,2},{4,3},{5,4},{6,5},{7,6},{8,7},{9,8},{10,9},{11,1... | collective-permute-start | bytes 393224 | tf_op jit(solution)/shard_map/ppermute | solution.py:73
  13.8 1.9 collective-permute-start
  15.7 0.8 copy.14
  16.5 0.7 copy-done.1
  17.2 0.7 copy-done.3
  17.9 6.5 %pair_inner.1 = (f32[128,2048]{1,0:T(8,128)S(1)}, f32[128,2048]{1,0:T(8,128)S(1)}, f32[128,2048]{1,0:T(8,128)S(1)}, f32[256,128]{1,0:T(8,128)S(1)}) custom-call(s32[16,3]{1,0:T(8,128)S(1)} %broadcast_subtract_fusion.col_ref, f32[128,2048]{1,0:T(8,128)S(1)} %constant_dynamic-update-slice_fusion.xp_ref, f32[16,3,128,128]{3,2,1,0:T(8,128)} %k_ref.11, ...), custom_call_target="tpu_custom_call" | custom-call | flops 2415919104 | bytes 6291456 | tf_op jit(solution)/shard_map/pair_inner/pallas_call | solution.py:500
  24.5 4.9 %collective-permute-done.low_ref = f32[128,256]{1,0:T(8,128)S(1)} collective-permute-done((f32[128,256]{1,0:T(8,128)S(1)}, f32[128,256]{1,0:T(8,128)S(1)}, u32[]{:S(2)}, u32[]{:S(2)}) %collective-permute-start) | collective-permute-done | bytes 131104 | tf_op jit(solution)/shard_map/ppermute | solution.py:72
  29.4 2.8 %pair_edges.1 = (f32[128,2048]{1,0:T(8,128)S(1)}, f32[128,2048]{1,0:T(8,128)S(1)}, f32[128,2048]{1,0:T(8,128)S(1)}, f32[192,128]{1,0:T(8,128)S(1)}) custom-call(s32[16,3]{1,0:T(8,128)S(1)} %broadcast_subtract_fusion.col_ref, f32[128,2048]{1,0:T(8,128)S(1)} %constant_dynamic-update-slice_fusion.xp_ref, ...), custom_call_target="tpu_custom_call", output_to_operand_aliasing={{0}: (5, {}), {1}: (6, {}), {2}: (7, {})} | custom-call | tf_op jit(solution)/shard_map/pair_edges/pallas_call | solution.py:507
  32.2 5.7 %collective-permute-start.3 = (f32[128,256]{1,0:T(8,128)S(1)}, f32[128,256]{1,0:T(8,128)S(1)}, u32[]{:S(2)}, u32[]{:S(2)}) collective-permute-start(f32[128,256]{1,0:T(8,128)S(1)} %get-tuple-element.70), channel_id=1, source_target_pairs={{1,0},{2,1},{3,2},{4,3},{5,4},{6,5},{7,6},{8,7},{9,8},{10,9},{11,1... | collective-permute-start | bytes 393224 | tf_op jit(solution)/shard_map/ppermute | solution.py:73
  37.9 4.1 %collective-permute-start.2 = (f32[128,256]{1,0:T(8,128)S(1)}, f32[128,256]{1,0:T(8,128)S(1)}, u32[]{:S(2)}, u32[]{:S(2)}) collective-permute-start(f32[128,256]{1,0:T(8,128)S(1)} %get-tuple-element.71), channel_id=1, source_target_pairs={{0,1},{1,2},{2,3},{3,4},{4,5},{5,6},{6,7},{7,8},{8,9},{9,10},{10,1... | collective-permute-start | bytes 393224 | tf_op jit(solution)/shard_map/ppermute | solution.py:72
  42.0 6.9 %parts_inner.1 = (f32[128,2048]{1,0:T(8,128)S(1)}, f32[128,2048]{1,0:T(8,128)S(1)}, f32[256,256]{1,0:T(8,128)S(1)}) custom-call(s32[16,3]{1,0:T(8,128)S(1)} %broadcast_subtract_fusion.col_ref, f32[128,2048]{1,0:T(8,128)S(1)} %constant_dynamic-update-slice_fusion.xp_ref, f32[128,2048]{1,0:T(8,128)S(1)} %get-tuple-element.40.parts_ref.s_ref, ...), custom_call_target="tpu_custom_call" | custom-call | flops 2415919104 | bytes 6291456 | tf_op jit(solution)/shard_map/parts_inner/pallas_call | solution.py:516
  48.9 4.1 %collective-permute-done.2.low_ref = f32[128,256]{1,0:T(8,128)S(1)} collective-permute-done((f32[128,256]{1,0:T(8,128)S(1)}, f32[128,256]{1,0:T(8,128)S(1)}, u32[]{:S(2)}, u32[]{:S(2)}) %collective-permute-start.2) | collective-permute-done | bytes 131104 | tf_op jit(solution)/shard_map/ppermute | solution.py:72
  53.0 3.0 %parts_edges.1 = (f32[128,2048]{1,0:T(8,128)S(1)}, f32[128,2048]{1,0:T(8,128)S(1)}, f32[160,128]{1,0:T(8,128)S(1)}, f32[160,128]{1,0:T(8,128)S(1)}, f32[160,128]{1,0:T(8,128)S(1)}, /*index=5*/f32[160,128]{1,0:T(8,128)S(1)}) custom-call(s32[16,3]{1,0:T(8,128)S(1)} %broadcast_subtract_fusion.col_ref, ...), custom_call_target="tpu_custom_call", output_to_operand_aliasing={{0}: (8, {}), {1}: (9, {})} | custom-call | tf_op jit(solution)/shard_map/parts_edges/pallas_call | solution.py:524
  56.2 2.9 %collective-permute-start.5 = (f32[160,128]{1,0:T(8,128)S(1)}, f32[160,128]{1,0:T(8,128)S(1)}, u32[]{:S(2)}, u32[]{:S(2)}) collective-permute-start(f32[160,128]{1,0:T(8,128)S(1)} %get-tuple-element.47), channel_id=1, source_target_pairs={{0,32},{1,33},{2,34},{3,35},{4,36},{5,37},{6,38},{7,39},{8,40},{9,... | collective-permute-start | bytes 245768 | tf_op jit(solution)/shard_map/ppermute | solution.py:35
  59.1 0.5 collective-permute-start.6
  59.7 1.0 collective-permute-done.4
  60.6 1.8 collective-permute-done.5
  62.4 1.1 collective-permute-done.6
  63.7 1.3 collective-permute-done.7
  65.0 0.4 collective-permute-start.10
  65.4 1.1 collective-permute-start.9
  66.5 2.6 %collective-permute-start.8 = (f32[160,128]{1,0:T(8,128)S(1)}, f32[160,128]{1,0:T(8,128)S(1)}, u32[]{:S(2)}, u32[]{:S(2)}) collective-permute-start(f32[160,128]{1,0:T(8,128)S(1)} %add.74), channel_id=1, source_target_pairs={{0,4},{1,5},{2,6},{3,7},{4,0},{5,1},{6,2},{7,3},{8,12},{9,13},{10,... | collective-permute-start | bytes 245768 | tf_op jit(solution)/shard_map/ppermute | solution.py:35
  69.1 3.4 %collective-permute-done.10 = f32[160,128]{1,0:T(8,128)S(1)} collective-permute-done((f32[160,128]{1,0:T(8,128)S(1)}, f32[160,128]{1,0:T(8,128)S(1)}, u32[]{:S(2)}, u32[]{:S(2)}) %collective-permute-start.10) | collective-permute-done | bytes 81952 | tf_op jit(solution)/shard_map/ppermute | solution.py:35
  72.5 0.6 collective-permute-done.8
  73.1 4.8 %collective-permute-start.13 = (f32[160,128]{1,0:T(8,128)S(1)}, f32[160,128]{1,0:T(8,128)S(1)}, u32[]{:S(2)}, u32[]{:S(2)}) collective-permute-start(f32[160,128]{1,0:T(8,128)S(1)} %add_add_fusion.4), channel_id=1, source_target_pairs={{0,192},{1,193},{2,194},{3,195},{4,196},{5,197},{6,198},{7,199},{8... | collective-permute-start | bytes 245768 | tf_op jit(solution)/shard_map/ppermute | solution.py:35
  77.9 0.7 collective-permute-start.11
  78.6 2.1 %collective-permute-done.13 = f32[160,128]{1,0:T(8,128)S(1)} collective-permute-done((f32[160,128]{1,0:T(8,128)S(1)}, f32[160,128]{1,0:T(8,128)S(1)}, u32[]{:S(2)}, u32[]{:S(2)}) %collective-permute-start.13) | collective-permute-done | bytes 81952 | tf_op jit(solution)/shard_map/ppermute | solution.py:35
  80.7 3.4 %collective-permute-done.12 = f32[160,128]{1,0:T(8,128)S(1)} collective-permute-done((f32[160,128]{1,0:T(8,128)S(1)}, f32[160,128]{1,0:T(8,128)S(1)}, u32[]{:S(2)}, u32[]{:S(2)}) %collective-permute-start.12) | collective-permute-done | bytes 81952 | tf_op jit(solution)/shard_map/ppermute | solution.py:35
  84.1 0.2 collective-permute-start.14
  84.3 8.3 %collective-permute-done.14 = f32[160,128]{1,0:T(8,128)S(1)} collective-permute-done((f32[160,128]{1,0:T(8,128)S(1)}, f32[160,128]{1,0:T(8,128)S(1)}, u32[]{:S(2)}, u32[]{:S(2)}) %collective-permute-start.14) | collective-permute-done | bytes 81952 | tf_op jit(solution)/shard_map/ppermute | solution.py:35
  92.7 0.3 collective-permute-start.17
  93.0 3.7 %collective-permute-start.16 = (f32[160,128]{1,0:T(8,128)S(1)}, f32[160,128]{1,0:T(8,128)S(1)}, u32[]{:S(2)}, u32[]{:S(2)}) collective-permute-start(f32[160,128]{1,0:T(8,128)S(1)} %add.81.refs_1_), channel_id=1, source_target_pairs={{0,32},{1,33},{2,34},{3,35},{4,36},{5,37},{6,38},{7,39},{8,40},{9,... | collective-permute-start | bytes 245768 | tf_op jit(solution)/shard_map/ppermute | solution.py:35
  96.7 0.6 collective-permute-start.15
  97.3 0.3 collective-permute-done.17.refs_4_
  97.6 1.8 collective-permute-done.16.refs_3_
  99.4 1.7 collective-permute-done.15.refs_2_
  101.2 27.7 %second_search.1 = (f32[64,2048]{1,0:T(8,128)S(1)}, f32[192,128]{1,0:T(8,128)S(1)}, f32[256,128]{1,0:T(8,128)S(1)}, f32[192,128]{1,0:T(8,128)S(1)}, f32[192,128]{1,0:T(8,128)S(1)}) custom-call(s32[1]{0:T(128)} %bitcast.at_ref.refs_0_, f32[160,128]{1,0:T(8,128)S(1)} %add.81.refs_1_, f32[160,128]{1,0:T(8,128)S(1)} %collective-permute-done.15.refs_2_, ...), custom_call_target="tpu_custom_call" | custom-call | tf_op jit(solution)/shard_map/second_search/pallas_call | solution.py:535
  128.9 0.7 mix_pair.1.xp_ref.refs_3_
  129.6 2.3 %collective-permute-start.19 = (f32[64,256]{1,0:T(8,128)S(1)}, f32[64,256]{1,0:T(8,128)S(1)}, u32[]{:S(2)}, u32[]{:S(2)}) collective-permute-start(f32[64,256]{1,0:T(8,128)S(1)} %get-tuple-element.74), channel_id=1, source_target_pairs={{1,0},{2,1},{3,2},{4,3},{5,4},{6,5},{7,6},{8,7},{9,8},{10,9},{11,1... | collective-permute-start | bytes 196616 | tf_op jit(solution)/shard_map/ppermute | solution.py:73
  131.9 7.5 %collective-permute-start.18 = (f32[64,256]{1,0:T(8,128)S(1)}, f32[64,256]{1,0:T(8,128)S(1)}, u32[]{:S(2)}, u32[]{:S(2)}) collective-permute-start(f32[64,256]{1,0:T(8,128)S(1)} %get-tuple-element.75), channel_id=1, source_target_pairs={{0,1},{1,2},{2,3},{3,4},{4,5},{5,6},{6,7},{7,8},{8,9},{9,10},{10,1... | collective-permute-start | bytes 196616 | tf_op jit(solution)/shard_map/ppermute | solution.py:72
  139.4 8.6 %second_inner.1.part_ref = f32[128,192]{1,0:T(8,128)S(1)} custom-call(s32[16,3]{1,0:T(8,128)S(1)} %broadcast_subtract_fusion.col_ref, f32[128,2048]{1,0:T(8,128)S(1)} %mix_pair.1.xp_ref.refs_3_, f32[64,2048]{1,0:T(8,128)S(1)} %get-tuple-element.54.s_ref.refs_4_, f32[16,3,128,128]{3,2,1,0:T(8,128)S(1)} %copy-done, f32[16,3,128,128]{3,2,1,0:T(8,128)} %m_ref.11, ...), custom_call_target="tpu_custom_call" | custom-call | flops 2415919104 | bytes 6291456 | tf_op jit(solution)/shard_map/second_inner/pallas_call | solution.py:552
  148.1 3.7 %second_edges.1 = f32[192,128]{1,0:T(8,128)S(1)} custom-call(s32[16,3]{1,0:T(8,128)S(1)} %broadcast_subtract_fusion.col_ref, f32[128,2048]{1,0:T(8,128)S(1)} %mix_pair.1.xp_ref.refs_3_, f32[64,2048]{1,0:T(8,128)S(1)} %get-tuple-element.54.s_ref.refs_4_, f32[64,256]{1,0:T(8,128)S(1)} %collective-permute-done.18.low_ref, ...), custom_call_target="tpu_custom_call" | custom-call | tf_op jit(solution)/shard_map/second_edges/pallas_call | solution.py:557
  151.9 1.3 collective-permute-done.20
  153.2 2.1 %collective-permute-start.23 = (f32[192,128]{1,0:T(8,128)S(1)}, f32[192,128]{1,0:T(8,128)S(1)}, u32[]{:S(2)}, u32[]{:S(2)}) collective-permute-start(f32[192,128]{1,0:T(8,128)S(1)} %add.82), channel_id=1, source_target_pairs={{0,48},{1,49},{2,50},{3,51},{4,52},{5,53},{6,54},{7,55},{8,56},{9,... | collective-permute-start | bytes 294920 | tf_op jit(solution)/shard_map/ppermute | solution.py:35
  155.3 2.1 %collective-permute-start.22 = (f32[192,128]{1,0:T(8,128)S(1)}, f32[192,128]{1,0:T(8,128)S(1)}, u32[]{:S(2)}, u32[]{:S(2)}) collective-permute-start(f32[192,128]{1,0:T(8,128)S(1)} %add.82), channel_id=1, source_target_pairs={{0,32},{1,33},{2,34},{3,35},{4,36},{5,37},{6,38},{7,39},{8,40},{9,... | collective-permute-start | bytes 294920 | tf_op jit(solution)/shard_map/ppermute | solution.py:35
  157.4 0.3 collective-permute-start.21
  157.7 1.3 collective-permute-done.23
  159.0 3.4 %collective-permute-done.22 = f32[192,128]{1,0:T(8,128)S(1)} collective-permute-done((f32[192,128]{1,0:T(8,128)S(1)}, f32[192,128]{1,0:T(8,128)S(1)}, u32[]{:S(2)}, u32[]{:S(2)}) %collective-permute-start.22) | collective-permute-done | bytes 98336 | tf_op jit(solution)/shard_map/ppermute | solution.py:35
  162.4 0.2 collective-permute-done.21
  162.7 1.7 collective-permute-start.26
  164.4 0.8 collective-permute-start.25
  165.2 1.7 collective-permute-start.24
  166.9 2.9 %collective-permute-done.26 = f32[192,128]{1,0:T(8,128)S(1)} collective-permute-done((f32[192,128]{1,0:T(8,128)S(1)}, f32[192,128]{1,0:T(8,128)S(1)}, u32[]{:S(2)}, u32[]{:S(2)}) %collective-permute-start.26) | collective-permute-done | bytes 98336 | tf_op jit(solution)/shard_map/ppermute | solution.py:35
  169.7 1.0 collective-permute-done.25
  170.8 2.0 collective-permute-start.29
  172.8 0.6 collective-permute-start.28
  173.4 1.8 collective-permute-start.27
  175.3 6.5 %next_first.1 = (f32[192,128]{1,0:T(8,128)S(1)}, f32[64,64]{1,0:T(8,128)S(1)}) custom-call(f32[192,128]{1,0:T(8,128)S(1)} %get-tuple-element.59.first_ref, f32[192,128]{1,0:T(8,128)S(1)} %get-tuple-element.60.second_ref, f32[192,128]{1,0:T(8,128)S(1)} %get-tuple-element.61.pair_ref), custom_call_target="tpu_custom_call" | custom-call | tf_op jit(solution)/shard_map/next_first/pallas_call | solution.py:546
  181.8 2.0 collective-permute-start.30
  183.8 6.1 %factor_pair.1.refs_2_ = f32[320,64]{1,0:T(8,128)S(1)} custom-call(f32[192,128]{1,0:T(8,128)S(1)} %get-tuple-element.67.first_ref.refs_0_, f32[64,64]{1,0:T(8,128)S(1)} %get-tuple-element.66.inv_ref), custom_call_target="tpu_custom_call" | custom-call | tf_op jit(solution)/shard_map/factor_pair/pallas_call | solution.py:543
  189.9 1.8 collective-permute-done.30
  191.7 15.0 %last_mix.1 = (f32[64,2048]{1,0:T(8,128)}, f32[64,2048]{1,0:T(8,128)}) custom-call(f32[192,128]{1,0:T(8,128)S(1)} %get-tuple-element.67.first_ref.refs_0_, f32[192,128]{1,0:T(8,128)S(1)} %add.92.refs_1_, f32[320,64]{1,0:T(8,128)S(1)} %factor_pair.1.refs_2_, f32[128,2048]{1,0:T(8,128)S(1)} %mix_pair.1.xp_ref.refs_3_, ...), custom_call_target="tpu_custom_call" | custom-call | tf_op jit(solution)/shard_map/last_mix/pallas_call | solution.py:565
  (34 shorter events, 0.6 us)
Async XLA Ops:
  2.8 21.6 %collective-permute-start.1 = (f32[128,256]{1,0:T(8,128)S(1)}, f32[128,256]{1,0:T(8,128)S(1)}, u32[]{:S(2)}, u32[]{:S(2)}) collective-permute-start(f32[128,256]{1,0:T(8,128)S(1)} %get-tuple-element.72), channel_id=1, source_target_pairs={{1,0},{2,1},{3,2},{4,3},{5,4},{6,5},{7,6},{8,7},{9,8},{10,9},{11,1... | collective-permute-start | bytes 393224 | tf_op jit(solution)/shard_map/ppermute | solution.py:73
  13.8 15.6 %collective-permute-start = (f32[128,256]{1,0:T(8,128)S(1)}, f32[128,256]{1,0:T(8,128)S(1)}, u32[]{:S(2)}, u32[]{:S(2)}) collective-permute-start(f32[128,256]{1,0:T(8,128)S(1)} %get-tuple-element.73), channel_id=1, source_target_pairs={{0,1},{1,2},{2,3},{3,4},{4,5},{5,6},{6,7},{7,8},{8,9},{9,10},{10,1... | collective-permute-start | bytes 393224 | tf_op jit(solution)/shard_map/ppermute | solution.py:72
  16.5 0.7 copy-start.1
  17.2 0.7 copy-start.3
  32.2 16.7 %collective-permute-start.3 = (f32[128,256]{1,0:T(8,128)S(1)}, f32[128,256]{1,0:T(8,128)S(1)}, u32[]{:S(2)}, u32[]{:S(2)}) collective-permute-start(f32[128,256]{1,0:T(8,128)S(1)} %get-tuple-element.70), channel_id=1, source_target_pairs={{1,0},{2,1},{3,2},{4,3},{5,4},{6,5},{7,6},{8,7},{9,8},{10,9},{11,1... | collective-permute-start | bytes 393224 | tf_op jit(solution)/shard_map/ppermute | solution.py:73
  37.9 15.1 %collective-permute-start.2 = (f32[128,256]{1,0:T(8,128)S(1)}, f32[128,256]{1,0:T(8,128)S(1)}, u32[]{:S(2)}, u32[]{:S(2)}) collective-permute-start(f32[128,256]{1,0:T(8,128)S(1)} %get-tuple-element.71), channel_id=1, source_target_pairs={{0,1},{1,2},{2,3},{3,4},{4,5},{5,6},{6,7},{7,8},{8,9},{9,10},{10,1... | collective-permute-start | bytes 393224 | tf_op jit(solution)/shard_map/ppermute | solution.py:72
  53.0 48.1 %copy-start.2 = (f32[2048]{0:T(1024)S(1)}, f32[2048]{0:T(1024)}, u32[]{:S(2)}) copy-start(f32[2048]{0:T(1024)} %param.12) | copy-start | bytes 24580
  56.1 4.5 %collective-permute-start.4 = (f32[160,128]{1,0:T(8,128)S(1)}, f32[160,128]{1,0:T(8,128)S(1)}, u32[]{:S(2)}, u32[]{:S(2)}) collective-permute-start(f32[160,128]{1,0:T(8,128)S(1)} %get-tuple-element.46), channel_id=1, source_target_pairs={{0,16},{1,17},{2,18},{3,19},{4,20},{5,21},{6,22},{7,23},{8,24},{9,... | collective-permute-start | bytes 245768 | tf_op jit(solution)/shard_map/ppermute | solution.py:35
  56.2 6.2 %collective-permute-start.5 = (f32[160,128]{1,0:T(8,128)S(1)}, f32[160,128]{1,0:T(8,128)S(1)}, u32[]{:S(2)}, u32[]{:S(2)}) collective-permute-start(f32[160,128]{1,0:T(8,128)S(1)} %get-tuple-element.47), channel_id=1, source_target_pairs={{0,32},{1,33},{2,34},{3,35},{4,36},{5,37},{6,38},{7,39},{8,40},{9,... | collective-permute-start | bytes 245768 | tf_op jit(solution)/shard_map/ppermute | solution.py:35
  59.1 4.4 %collective-permute-start.6 = (f32[160,128]{1,0:T(8,128)S(1)}, f32[160,128]{1,0:T(8,128)S(1)}, u32[]{:S(2)}, u32[]{:S(2)}) collective-permute-start(f32[160,128]{1,0:T(8,128)S(1)} %get-tuple-element.48), channel_id=1, source_target_pairs={{0,48},{1,49},{2,50},{3,51},{4,52},{5,53},{6,54},{7,55},{8,56},{9,... | collective-permute-start | bytes 245768 | tf_op jit(solution)/shard_map/ppermute | solution.py:35
  63.6 1.4 collective-permute-start.7
  65.0 7.6 %collective-permute-start.10 = (f32[160,128]{1,0:T(8,128)S(1)}, f32[160,128]{1,0:T(8,128)S(1)}, u32[]{:S(2)}, u32[]{:S(2)}) collective-permute-start(f32[160,128]{1,0:T(8,128)S(1)} %add.74), channel_id=1, source_target_pairs={{0,12},{1,13},{2,14},{3,15},{4,8},{5,9},{6,10},{7,11},{8,4},{9,5},... | collective-permute-start | bytes 245768 | tf_op jit(solution)/shard_map/ppermute | solution.py:35
  65.4 7.1 %collective-permute-start.9 = (f32[160,128]{1,0:T(8,128)S(1)}, f32[160,128]{1,0:T(8,128)S(1)}, u32[]{:S(2)}, u32[]{:S(2)}) collective-permute-start(f32[160,128]{1,0:T(8,128)S(1)} %add.74), channel_id=1, source_target_pairs={{0,8},{1,9},{2,10},{3,11},{4,12},{5,13},{6,14},{7,15},{8,0},{9,1},... | collective-permute-start | bytes 245768 | tf_op jit(solution)/shard_map/ppermute | solution.py:35
  66.5 6.6 %collective-permute-start.8 = (f32[160,128]{1,0:T(8,128)S(1)}, f32[160,128]{1,0:T(8,128)S(1)}, u32[]{:S(2)}, u32[]{:S(2)}) collective-permute-start(f32[160,128]{1,0:T(8,128)S(1)} %add.74), channel_id=1, source_target_pairs={{0,4},{1,5},{2,6},{3,7},{4,0},{5,1},{6,2},{7,3},{8,12},{9,13},{10,... | collective-permute-start | bytes 245768 | tf_op jit(solution)/shard_map/ppermute | solution.py:35
  73.1 7.6 %collective-permute-start.13 = (f32[160,128]{1,0:T(8,128)S(1)}, f32[160,128]{1,0:T(8,128)S(1)}, u32[]{:S(2)}, u32[]{:S(2)}) collective-permute-start(f32[160,128]{1,0:T(8,128)S(1)} %add_add_fusion.4), channel_id=1, source_target_pairs={{0,192},{1,193},{2,194},{3,195},{4,196},{5,197},{6,198},{7,199},{8... | collective-permute-start | bytes 245768 | tf_op jit(solution)/shard_map/ppermute | solution.py:35
  77.9 6.2 %collective-permute-start.12 = (f32[160,128]{1,0:T(8,128)S(1)}, f32[160,128]{1,0:T(8,128)S(1)}, u32[]{:S(2)}, u32[]{:S(2)}) collective-permute-start(f32[160,128]{1,0:T(8,128)S(1)} %add_add_fusion.4), channel_id=1, source_target_pairs={{0,128},{1,129},{2,130},{3,131},{4,132},{5,133},{6,134},{7,135},{8... | collective-permute-start | bytes 245768 | tf_op jit(solution)/shard_map/ppermute | solution.py:35
  77.9 6.2 %collective-permute-start.11 = (f32[160,128]{1,0:T(8,128)S(1)}, f32[160,128]{1,0:T(8,128)S(1)}, u32[]{:S(2)}, u32[]{:S(2)}) collective-permute-start(f32[160,128]{1,0:T(8,128)S(1)} %add_add_fusion.4), channel_id=1, source_target_pairs={{0,64},{1,65},{2,66},{3,67},{4,68},{5,69},{6,70},{7,71},{8,72},{9,... | collective-permute-start | bytes 245768 | tf_op jit(solution)/shard_map/ppermute | solution.py:35
  84.1 8.5 %collective-permute-start.14 = (f32[160,128]{1,0:T(8,128)S(1)}, f32[160,128]{1,0:T(8,128)S(1)}, u32[]{:S(2)}, u32[]{:S(2)}) collective-permute-start(f32[160,128]{1,0:T(8,128)S(1)} %add_add_fusion.3), channel_id=1, source_target_pairs={{0,1},{1,0},{2,3},{3,2},{4,5},{5,4},{6,7},{7,6},{8,9},{9,8},{10,11... | collective-permute-start | bytes 245768 | tf_op jit(solution)/shard_map/ppermute | solution.py:35
  92.7 4.9 %collective-permute-start.17 = (f32[160,128]{1,0:T(8,128)S(1)}, f32[160,128]{1,0:T(8,128)S(1)}, u32[]{:S(2)}, u32[]{:S(2)}) collective-permute-start(f32[160,128]{1,0:T(8,128)S(1)} %add.81.refs_1_), channel_id=1, source_target_pairs={{0,48},{1,49},{2,50},{3,51},{4,52},{5,53},{6,54},{7,55},{8,56},{9,... | collective-permute-start | bytes 245768 | tf_op jit(solution)/shard_map/ppermute | solution.py:35
  93.0 6.4 %collective-permute-start.16 = (f32[160,128]{1,0:T(8,128)S(1)}, f32[160,128]{1,0:T(8,128)S(1)}, u32[]{:S(2)}, u32[]{:S(2)}) collective-permute-start(f32[160,128]{1,0:T(8,128)S(1)} %add.81.refs_1_), channel_id=1, source_target_pairs={{0,32},{1,33},{2,34},{3,35},{4,36},{5,37},{6,38},{7,39},{8,40},{9,... | collective-permute-start | bytes 245768 | tf_op jit(solution)/shard_map/ppermute | solution.py:35
  96.7 4.4 %collective-permute-start.15 = (f32[160,128]{1,0:T(8,128)S(1)}, f32[160,128]{1,0:T(8,128)S(1)}, u32[]{:S(2)}, u32[]{:S(2)}) collective-permute-start(f32[160,128]{1,0:T(8,128)S(1)} %add.81.refs_1_), channel_id=1, source_target_pairs={{0,16},{1,17},{2,18},{3,19},{4,20},{5,21},{6,22},{7,23},{8,24},{9,... | collective-permute-start | bytes 245768 | tf_op jit(solution)/shard_map/ppermute | solution.py:35
  101.2 38.2 %copy-start = (f32[16,3,128,128]{3,2,1,0:T(8,128)S(1)}, f32[16,3,128,128]{3,2,1,0:T(8,128)}, u32[]{:S(2)}) copy-start(f32[16,3,128,128]{3,2,1,0:T(8,128)} %k_ref.11) | copy-start | bytes 9437188
  129.6 18.4 %collective-permute-start.19 = (f32[64,256]{1,0:T(8,128)S(1)}, f32[64,256]{1,0:T(8,128)S(1)}, u32[]{:S(2)}, u32[]{:S(2)}) collective-permute-start(f32[64,256]{1,0:T(8,128)S(1)} %get-tuple-element.74), channel_id=1, source_target_pairs={{1,0},{2,1},{3,2},{4,3},{5,4},{6,5},{7,6},{8,7},{9,8},{10,9},{11,1... | collective-permute-start | bytes 196616 | tf_op jit(solution)/shard_map/ppermute | solution.py:73
  131.9 16.2 %collective-permute-start.18 = (f32[64,256]{1,0:T(8,128)S(1)}, f32[64,256]{1,0:T(8,128)S(1)}, u32[]{:S(2)}, u32[]{:S(2)}) collective-permute-start(f32[64,256]{1,0:T(8,128)S(1)} %get-tuple-element.75), channel_id=1, source_target_pairs={{0,1},{1,2},{2,3},{3,4},{4,5},{5,6},{6,7},{7,8},{8,9},{9,10},{10,1... | collective-permute-start | bytes 196616 | tf_op jit(solution)/shard_map/ppermute | solution.py:72
  151.8 1.4 collective-permute-start.20
  153.2 5.8 %collective-permute-start.23 = (f32[192,128]{1,0:T(8,128)S(1)}, f32[192,128]{1,0:T(8,128)S(1)}, u32[]{:S(2)}, u32[]{:S(2)}) collective-permute-start(f32[192,128]{1,0:T(8,128)S(1)} %add.82), channel_id=1, source_target_pairs={{0,48},{1,49},{2,50},{3,51},{4,52},{5,53},{6,54},{7,55},{8,56},{9,... | collective-permute-start | bytes 294920 | tf_op jit(solution)/shard_map/ppermute | solution.py:35
  155.3 7.1 %collective-permute-start.22 = (f32[192,128]{1,0:T(8,128)S(1)}, f32[192,128]{1,0:T(8,128)S(1)}, u32[]{:S(2)}, u32[]{:S(2)}) collective-permute-start(f32[192,128]{1,0:T(8,128)S(1)} %add.82), channel_id=1, source_target_pairs={{0,32},{1,33},{2,34},{3,35},{4,36},{5,37},{6,38},{7,39},{8,40},{9,... | collective-permute-start | bytes 294920 | tf_op jit(solution)/shard_map/ppermute | solution.py:35
  157.4 5.2 %collective-permute-start.21 = (f32[192,128]{1,0:T(8,128)S(1)}, f32[192,128]{1,0:T(8,128)S(1)}, u32[]{:S(2)}, u32[]{:S(2)}) collective-permute-start(f32[192,128]{1,0:T(8,128)S(1)} %add.82), channel_id=1, source_target_pairs={{0,16},{1,17},{2,18},{3,19},{4,20},{5,21},{6,22},{7,23},{8,24},{9,... | collective-permute-start | bytes 294920 | tf_op jit(solution)/shard_map/ppermute | solution.py:35
  162.7 7.1 %collective-permute-start.26 = (f32[192,128]{1,0:T(8,128)S(1)}, f32[192,128]{1,0:T(8,128)S(1)}, u32[]{:S(2)}, u32[]{:S(2)}) collective-permute-start(f32[192,128]{1,0:T(8,128)S(1)} %add_add_fusion.2), channel_id=1, source_target_pairs={{0,12},{1,13},{2,14},{3,15},{4,8},{5,9},{6,10},{7,11},{8,4},{9,5},... | collective-permute-start | bytes 294920 | tf_op jit(solution)/shard_map/ppermute | solution.py:35
  164.4 6.3 %collective-permute-start.25 = (f32[192,128]{1,0:T(8,128)S(1)}, f32[192,128]{1,0:T(8,128)S(1)}, u32[]{:S(2)}, u32[]{:S(2)}) collective-permute-start(f32[192,128]{1,0:T(8,128)S(1)} %add_add_fusion.2), channel_id=1, source_target_pairs={{0,8},{1,9},{2,10},{3,11},{4,12},{5,13},{6,14},{7,15},{8,0},{9,1},... | collective-permute-start | bytes 294920 | tf_op jit(solution)/shard_map/ppermute | solution.py:35
  165.2 5.6 %collective-permute-start.24 = (f32[192,128]{1,0:T(8,128)S(1)}, f32[192,128]{1,0:T(8,128)S(1)}, u32[]{:S(2)}, u32[]{:S(2)}) collective-permute-start(f32[192,128]{1,0:T(8,128)S(1)} %add_add_fusion.2), channel_id=1, source_target_pairs={{0,4},{1,5},{2,6},{3,7},{4,0},{5,1},{6,2},{7,3},{8,12},{9,13},{10,... | collective-permute-start | bytes 294920 | tf_op jit(solution)/shard_map/ppermute | solution.py:35
  170.8 10.9 %collective-permute-start.29 = (f32[192,128]{1,0:T(8,128)S(1)}, f32[192,128]{1,0:T(8,128)S(1)}, u32[]{:S(2)}, u32[]{:S(2)}) collective-permute-start(f32[192,128]{1,0:T(8,128)S(1)} %add_add_fusion.1), channel_id=1, source_target_pairs={{0,192},{1,193},{2,194},{3,195},{4,196},{5,197},{6,198},{7,199},{8... | collective-permute-start | bytes 294920 | tf_op jit(solution)/shard_map/ppermute | solution.py:35
  172.8 8.9 %collective-permute-start.28 = (f32[192,128]{1,0:T(8,128)S(1)}, f32[192,128]{1,0:T(8,128)S(1)}, u32[]{:S(2)}, u32[]{:S(2)}) collective-permute-start(f32[192,128]{1,0:T(8,128)S(1)} %add_add_fusion.1), channel_id=1, source_target_pairs={{0,128},{1,129},{2,130},{3,131},{4,132},{5,133},{6,134},{7,135},{8... | collective-permute-start | bytes 294920 | tf_op jit(solution)/shard_map/ppermute | solution.py:35
  173.4 8.3 %collective-permute-start.27 = (f32[192,128]{1,0:T(8,128)S(1)}, f32[192,128]{1,0:T(8,128)S(1)}, u32[]{:S(2)}, u32[]{:S(2)}) collective-permute-start(f32[192,128]{1,0:T(8,128)S(1)} %add_add_fusion.1), channel_id=1, source_target_pairs={{0,64},{1,65},{2,66},{3,67},{4,68},{5,69},{6,70},{7,71},{8,72},{9,... | collective-permute-start | bytes 294920 | tf_op jit(solution)/shard_map/ppermute | solution.py:35
  181.8 9.9 %collective-permute-start.30 = (f32[192,128]{1,0:T(8,128)S(1)}, f32[192,128]{1,0:T(8,128)S(1)}, u32[]{:S(2)}, u32[]{:S(2)}) collective-permute-start(f32[192,128]{1,0:T(8,128)S(1)} %add_add_fusion), channel_id=1, source_target_pairs={{0,1},{1,0},{2,3},{3,2},{4,5},{5,4},{6,7},{7,6},{8,9},{9,8},{10,11... | collective-permute-start | bytes 294920 | tf_op jit(solution)/shard_map/ppermute | solution.py:35
where the time goes:
time: 207 us
  Pallas kernels  87.7 us (42%)
  starting transfers between devices  65.7 us (32%)
  waiting for transfers between devices  47.8 us (23%)
  local copies, waits for them, and re-layouts  4.37 us (2%)
    ppermute x25, waiting for transfers between devices, partner(): return lax.ppermute(x, AXES, pairs)  38.8 us
    ppermute x25, starting transfers between devices, partner(): return lax.ppermute(x, AXES, pairs)  33.4 us
    pallas_call x1, Pallas kernels, shards(): call(lambda *refs: second_search(total_rows, *refs), 'second_search', [sm...  27.7 us
    ppermute x3, starting transfers between devices, exchange(): lax.ppermute(head, AXES, [(i + 1, i) for i in range(count - 1)])  18.9 us
    pallas_call x1, Pallas kernels, shards(): call(lambda *refs: last_kernel(total_rows, *refs), 'last_mix', [whole()]...  15 us
    ppermute x3, starting transfers between devices, exchange(): low = lax.ppermute(tail, AXES, [(i, i + 1) for i in range(count - 1)])  13.5 us
    ppermute x3, waiting for transfers between devices, exchange(): low = lax.ppermute(tail, AXES, [(i, i + 1) for i in range(count - 1)])  9 us
    pallas_call x1, Pallas kernels, shards(): call(search_inner, 'second_inner', [smem()] + [whole()] * 2 + stored(insi...  8.65 us
  transfers between devices with their start and end apart: 31, of which 21 were waited for; matrix products, arithmetic and copies ran while one was open for 0% of the time, Pallas kernels for 17%

commit v1 on v0

--- a/solution.py
+++ b/solution.py
@@ -12,6 +12,7 @@
 AXES = ("slab", "row")
 HIGHEST = lax.Precision.HIGHEST
 STEP = 2
+PANEL = 8
 QUARTER = 160
 VMEM_LIMIT = 48 * 1024 * 1024
 
@@ -99,21 +100,26 @@
 
 
 def factor_inverses(mats):
-    rows = lax.broadcasted_iota(jnp.int32, (COLS, 1), 0)
     eye = (
         lax.broadcasted_iota(jnp.int32, (COLS, COLS), 0) == lax.broadcasted_iota(jnp.int32, (COLS, COLS), 1)
     ).astype(jnp.float32)
     work = [jnp.concatenate([a, eye], 1) for a in mats]
-    for j in range(0, COLS, 2):
+    done = [[] for _ in mats]
+    for p in range(0, COLS, PANEL):
+        left = COLS - p
+        rows = lax.broadcasted_iota(jnp.int32, (left, 2 * COLS), 0)
         for n, w in enumerate(work):
-            r1, r2 = w[j : j + 1, :], w[j + 1 : j + 2, :]
-            a, b, c = r1[:, j : j + 1], r1[:, j + 1 : j + 2], r2[:, j + 1 : j + 2]
-            scale = 1.0 / (a * c - b * b)
-            u1, u2 = (c * r1 - b * r2) * scale, (a * r2 - b * r1) * scale
-            below = w[:, j : j + 1] * u1 + w[:, j + 1 : j + 2] * u2
-            work[n] = w - jnp.where(rows > j + 1, below, jnp.where(rows == j + 1, (b / a) * r1, 0.0))
+            cols = [jnp.broadcast_to(w[:, p + k : p + k + 1], (left, 2 * COLS)) for k in range(PANEL)]
+            for j in range(PANEL):
+                factor = jnp.where(rows > j, cols[j] * (1.0 / cols[j][j : j + 1, :]), 0.0)
+                for k in range(j + 1, PANEL):
+                    cols[k] = cols[k] - factor * cols[k][j : j + 1, :]
+                w = w - factor * w[j : j + 1, :]
+            done[n].append(w[:PANEL])
+            work[n] = w[PANEL:]
     out = []
-    for w in work:
+    for parts in done:
+        w = jnp.concatenate(parts, 0)
         d = jnp.sum(w[:, :COLS] * eye, axis=1, keepdims=True)
         r = lax.rsqrt(d)
         r = r * (1.5 - 0.5 * d * r * r)

time: 207 us -> 186 us (0.90)
  Pallas kernels: 87.7 us -> 61.3 us
  waiting for transfers between devices: 47.8 us -> 53.5 us
    pallas_call x1, Pallas kernels: 27.7 us -> 14.8 us  [shards(): call(lambda *refs: second_search(total_rows, *refs), 'second_search', [sm...]
    pallas_call x1, Pallas kernels: 15 us -> 8.37 us  [shards(): call(lambda *refs: last_kernel(total_rows, *refs), 'last_mix', [whole()]...]
    ppermute x25, waiting for transfers between devices: 38.8 us -> 44.5 us  [partner(): return lax.ppermute(x, AXES, pairs)]
    pallas_call x1, Pallas kernels: 6.46 us -> 2.98 us  [grams(): call(next_first, 'next_first', [whole()] * 3, [whole()] * 2, [f32(192, 12...]
    pallas_call x1, Pallas kernels: 6.11 us -> 2.75 us  [factor(): call(factor_pair, 'factor_pair', [whole()] * 2, whole(), f32(320, 64))]
  transfers between devices with their start and end apart: 31 -> 31, of which waited for: 21 -> 22; matrix products, arithmetic and copies ran while one was open for 0% -> 0% of each run, Pallas kernels for 17% -> 15%
where the time goes in v1:
time: 186 us
  starting transfers between devices  65.4 us (35%)
  Pallas kernels  61.3 us (33%)
  waiting for transfers between devices  53.5 us (29%)
  local copies, waits for them, and re-layouts  4.37 us (2%)
    ppermute x25, waiting for transfers between devices, partner(): return lax.ppermute(x, AXES, pairs)  44.5 us
    ppermute x25, starting transfers between devices, partner(): return lax.ppermute(x, AXES, pairs)  33.1 us
    ppermute x3, starting transfers between devices, exchange(): lax.ppermute(head, AXES, [(i + 1, i) for i in range(count - 1)])  18.9 us
    pallas_call x1, Pallas kernels, shards(): call(lambda *refs: second_search(total_rows, *refs), 'second_search', [sm...  14.8 us
    ppermute x3, starting transfers between devices, exchange(): low = lax.ppermute(tail, AXES, [(i, i + 1) for i in range(count - 1)])  13.5 us
    ppermute x3, waiting for transfers between devices, exchange(): low = lax.ppermute(tail, AXES, [(i, i + 1) for i in range(count - 1)])  9 us
    pallas_call x1, Pallas kernels, shards(): call(search_inner, 'second_inner', [smem()] + [whole()] * 2 + stored(insi...  8.65 us
    pallas_call x1, Pallas kernels, shards(): call(lambda *refs: last_kernel(total_rows, *refs), 'last_mix', [whole()]...  8.37 us
  transfers between devices with their start and end apart: 31, of which 22 were waited for; matrix products, arithmetic and copies ran while one was open for 0% of the time, Pallas kernels for 15%

profile of v1, /device:TPU:2, one launch (start us, length us, event | category | flops | bytes accessed | tf_op | source)
XLA Modules:
  0.0 185.7 jit_solution(11343218661472891948)
XLA Ops:
  0.6 1.1 constant_dynamic-update-slice_fusion.1
  1.7 1.1 constant_dynamic-update-slice_fusion.xp_ref
  2.8 11.0 %collective-permute-start.1 = (f32[128,256]{1,0:T(8,128)S(1)}, f32[128,256]{1,0:T(8,128)S(1)}, u32[]{:S(2)}, u32[]{:S(2)}) collective-permute-start(f32[128,256]{1,0:T(8,128)S(1)} %get-tuple-element.72), channel_id=1, source_target_pairs={{1,0},{2,1},{3,2},{4,3},{5,4},{6,5},{7,6},{8,7},{9,8},{10,9},{11,1... | collective-permute-start | bytes 393224 | tf_op jit(solution)/shard_map/ppermute | solution.py:74
  13.8 1.9 %collective-permute-start = (f32[128,256]{1,0:T(8,128)S(1)}, f32[128,256]{1,0:T(8,128)S(1)}, u32[]{:S(2)}, u32[]{:S(2)}) collective-permute-start(f32[128,256]{1,0:T(8,128)S(1)} %get-tuple-element.73), channel_id=1, source_target_pairs={{0,1},{1,2},{2,3},{3,4},{4,5},{5,6},{6,7},{7,8},{8,9},{9,10},{10,1... | collective-permute-start | bytes 393224 | tf_op jit(solution)/shard_map/ppermute | solution.py:73
  15.7 0.8 copy.14
  16.5 0.7 copy-done.1
  17.2 0.7 copy-done.3
  17.9 6.5 %pair_inner.1 = (f32[128,2048]{1,0:T(8,128)S(1)}, f32[128,2048]{1,0:T(8,128)S(1)}, f32[128,2048]{1,0:T(8,128)S(1)}, f32[256,128]{1,0:T(8,128)S(1)}) custom-call(s32[16,3]{1,0:T(8,128)S(1)} %broadcast_subtract_fusion.col_ref, f32[128,2048]{1,0:T(8,128)S(1)} %constant_dynamic-update-slice_fusion.xp_ref, f32[16,3,128,128]{3,2,1,0:T(8,128)} %k_ref.11, ...), custom_call_target="tpu_custom_call" | custom-call | flops 2415919104 | bytes 6291456 | tf_op jit(solution)/shard_map/pair_inner/pallas_call | solution.py:506
  24.5 4.9 %collective-permute-done.low_ref = f32[128,256]{1,0:T(8,128)S(1)} collective-permute-done((f32[128,256]{1,0:T(8,128)S(1)}, f32[128,256]{1,0:T(8,128)S(1)}, u32[]{:S(2)}, u32[]{:S(2)}) %collective-permute-start) | collective-permute-done | bytes 131104 | tf_op jit(solution)/shard_map/ppermute | solution.py:73
  29.4 2.8 %pair_edges.1 = (f32[128,2048]{1,0:T(8,128)S(1)}, f32[128,2048]{1,0:T(8,128)S(1)}, f32[128,2048]{1,0:T(8,128)S(1)}, f32[192,128]{1,0:T(8,128)S(1)}) custom-call(s32[16,3]{1,0:T(8,128)S(1)} %broadcast_subtract_fusion.col_ref, f32[128,2048]{1,0:T(8,128)S(1)} %constant_dynamic-update-slice_fusion.xp_ref, ...), custom_call_target="tpu_custom_call", output_to_operand_aliasing={{0}: (5, {}), {1}: (6, {}), {2}: (7, {})} | custom-call | tf_op jit(solution)/shard_map/pair_edges/pallas_call | solution.py:513
  32.2 5.7 %collective-permute-start.3 = (f32[128,256]{1,0:T(8,128)S(1)}, f32[128,256]{1,0:T(8,128)S(1)}, u32[]{:S(2)}, u32[]{:S(2)}) collective-permute-start(f32[128,256]{1,0:T(8,128)S(1)} %get-tuple-element.70), channel_id=1, source_target_pairs={{1,0},{2,1},{3,2},{4,3},{5,4},{6,5},{7,6},{8,7},{9,8},{10,9},{11,1... | collective-permute-start | bytes 393224 | tf_op jit(solution)/shard_map/ppermute | solution.py:74
  37.9 4.1 %collective-permute-start.2 = (f32[128,256]{1,0:T(8,128)S(1)}, f32[128,256]{1,0:T(8,128)S(1)}, u32[]{:S(2)}, u32[]{:S(2)}) collective-permute-start(f32[128,256]{1,0:T(8,128)S(1)} %get-tuple-element.71), channel_id=1, source_target_pairs={{0,1},{1,2},{2,3},{3,4},{4,5},{5,6},{6,7},{7,8},{8,9},{9,10},{10,1... | collective-permute-start | bytes 393224 | tf_op jit(solution)/shard_map/ppermute | solution.py:73
  42.0 6.9 %parts_inner.1 = (f32[128,2048]{1,0:T(8,128)S(1)}, f32[128,2048]{1,0:T(8,128)S(1)}, f32[256,256]{1,0:T(8,128)S(1)}) custom-call(s32[16,3]{1,0:T(8,128)S(1)} %broadcast_subtract_fusion.col_ref, f32[128,2048]{1,0:T(8,128)S(1)} %constant_dynamic-update-slice_fusion.xp_ref, f32[128,2048]{1,0:T(8,128)S(1)} %get-tuple-element.40.parts_ref.s_ref, ...), custom_call_target="tpu_custom_call" | custom-call | flops 2415919104 | bytes 6291456 | tf_op jit(solution)/shard_map/parts_inner/pallas_call | solution.py:522
  48.9 4.1 %collective-permute-done.2.low_ref = f32[128,256]{1,0:T(8,128)S(1)} collective-permute-done((f32[128,256]{1,0:T(8,128)S(1)}, f32[128,256]{1,0:T(8,128)S(1)}, u32[]{:S(2)}, u32[]{:S(2)}) %collective-permute-start.2) | collective-permute-done | bytes 131104 | tf_op jit(solution)/shard_map/ppermute | solution.py:73
  53.0 3.0 %parts_edges.1 = (f32[128,2048]{1,0:T(8,128)S(1)}, f32[128,2048]{1,0:T(8,128)S(1)}, f32[160,128]{1,0:T(8,128)S(1)}, f32[160,128]{1,0:T(8,128)S(1)}, f32[160,128]{1,0:T(8,128)S(1)}, /*index=5*/f32[160,128]{1,0:T(8,128)S(1)}) custom-call(s32[16,3]{1,0:T(8,128)S(1)} %broadcast_subtract_fusion.col_ref, ...), custom_call_target="tpu_custom_call", output_to_operand_aliasing={{0}: (8, {}), {1}: (9, {})} | custom-call | tf_op jit(solution)/shard_map/parts_edges/pallas_call | solution.py:530
  56.2 2.9 %collective-permute-start.5 = (f32[160,128]{1,0:T(8,128)S(1)}, f32[160,128]{1,0:T(8,128)S(1)}, u32[]{:S(2)}, u32[]{:S(2)}) collective-permute-start(f32[160,128]{1,0:T(8,128)S(1)} %get-tuple-element.47), channel_id=1, source_target_pairs={{0,32},{1,33},{2,34},{3,35},{4,36},{5,37},{6,38},{7,39},{8,40},{9,... | collective-permute-start | bytes 245768 | tf_op jit(solution)/shard_map/ppermute | solution.py:36
  59.1 0.5 collective-permute-start.6
  59.7 1.0 collective-permute-done.4
  60.6 1.8 collective-permute-done.5
  62.4 1.1 collective-permute-done.6
  63.7 1.3 collective-permute-done.7
  65.0 0.4 collective-permute-start.10
  65.4 1.1 collective-permute-start.9
  66.5 2.6 %collective-permute-start.8 = (f32[160,128]{1,0:T(8,128)S(1)}, f32[160,128]{1,0:T(8,128)S(1)}, u32[]{:S(2)}, u32[]{:S(2)}) collective-permute-start(f32[160,128]{1,0:T(8,128)S(1)} %add.74), channel_id=1, source_target_pairs={{0,4},{1,5},{2,6},{3,7},{4,0},{5,1},{6,2},{7,3},{8,12},{9,13},{10,... | collective-permute-start | bytes 245768 | tf_op jit(solution)/shard_map/ppermute | solution.py:36
  69.1 3.4 %collective-permute-done.10 = f32[160,128]{1,0:T(8,128)S(1)} collective-permute-done((f32[160,128]{1,0:T(8,128)S(1)}, f32[160,128]{1,0:T(8,128)S(1)}, u32[]{:S(2)}, u32[]{:S(2)}) %collective-permute-start.10) | collective-permute-done | bytes 81952 | tf_op jit(solution)/shard_map/ppermute | solution.py:36
  72.5 0.6 collective-permute-done.8
  73.1 4.8 %collective-permute-start.13 = (f32[160,128]{1,0:T(8,128)S(1)}, f32[160,128]{1,0:T(8,128)S(1)}, u32[]{:S(2)}, u32[]{:S(2)}) collective-permute-start(f32[160,128]{1,0:T(8,128)S(1)} %add_add_fusion.4), channel_id=1, source_target_pairs={{0,192},{1,193},{2,194},{3,195},{4,196},{5,197},{6,198},{7,199},{8... | collective-permute-start | bytes 245768 | tf_op jit(solution)/shard_map/ppermute | solution.py:36
  77.9 0.7 collective-permute-start.11
  78.6 2.1 %collective-permute-done.13 = f32[160,128]{1,0:T(8,128)S(1)} collective-permute-done((f32[160,128]{1,0:T(8,128)S(1)}, f32[160,128]{1,0:T(8,128)S(1)}, u32[]{:S(2)}, u32[]{:S(2)}) %collective-permute-start.13) | collective-permute-done | bytes 81952 | tf_op jit(solution)/shard_map/ppermute | solution.py:36
  80.7 3.4 %collective-permute-done.12 = f32[160,128]{1,0:T(8,128)S(1)} collective-permute-done((f32[160,128]{1,0:T(8,128)S(1)}, f32[160,128]{1,0:T(8,128)S(1)}, u32[]{:S(2)}, u32[]{:S(2)}) %collective-permute-start.12) | collective-permute-done | bytes 81952 | tf_op jit(solution)/shard_map/ppermute | solution.py:36
  84.3 8.3 %collective-permute-done.14 = f32[160,128]{1,0:T(8,128)S(1)} collective-permute-done((f32[160,128]{1,0:T(8,128)S(1)}, f32[160,128]{1,0:T(8,128)S(1)}, u32[]{:S(2)}, u32[]{:S(2)}) %collective-permute-start.14) | collective-permute-done | bytes 81952 | tf_op jit(solution)/shard_map/ppermute | solution.py:36
  92.7 0.3 collective-permute-start.17
  93.0 3.7 %collective-permute-start.16 = (f32[160,128]{1,0:T(8,128)S(1)}, f32[160,128]{1,0:T(8,128)S(1)}, u32[]{:S(2)}, u32[]{:S(2)}) collective-permute-start(f32[160,128]{1,0:T(8,128)S(1)} %add.81.refs_1_), channel_id=1, source_target_pairs={{0,32},{1,33},{2,34},{3,35},{4,36},{5,37},{6,38},{7,39},{8,40},{9,... | collective-permute-start | bytes 245768 | tf_op jit(solution)/shard_map/ppermute | solution.py:36
  96.7 0.6 collective-permute-start.15
  97.3 0.3 collective-permute-done.17.refs_4_
  97.6 1.8 collective-permute-done.16.refs_3_
  99.4 1.7 collective-permute-done.15.refs_2_
  101.2 14.8 %second_search.1 = (f32[64,2048]{1,0:T(8,128)S(1)}, f32[192,128]{1,0:T(8,128)S(1)}, f32[256,128]{1,0:T(8,128)S(1)}, f32[192,128]{1,0:T(8,128)S(1)}, f32[192,128]{1,0:T(8,128)S(1)}) custom-call(s32[1]{0:T(128)} %bitcast.at_ref.refs_0_, f32[160,128]{1,0:T(8,128)S(1)} %add.81.refs_1_, f32[160,128]{1,0:T(8,128)S(1)} %collective-permute-done.15.refs_2_, ...), custom_call_target="tpu_custom_call" | custom-call | tf_op jit(solution)/shard_map/second_search/pallas_call | solution.py:541
  115.9 0.7 mix_pair.1.xp_ref.refs_3_
  116.7 2.3 %collective-permute-start.19 = (f32[64,256]{1,0:T(8,128)S(1)}, f32[64,256]{1,0:T(8,128)S(1)}, u32[]{:S(2)}, u32[]{:S(2)}) collective-permute-start(f32[64,256]{1,0:T(8,128)S(1)} %get-tuple-element.74), channel_id=1, source_target_pairs={{1,0},{2,1},{3,2},{4,3},{5,4},{6,5},{7,6},{8,7},{9,8},{10,9},{11,1... | collective-permute-start | bytes 196616 | tf_op jit(solution)/shard_map/ppermute | solution.py:74
  119.0 7.5 %collective-permute-start.18 = (f32[64,256]{1,0:T(8,128)S(1)}, f32[64,256]{1,0:T(8,128)S(1)}, u32[]{:S(2)}, u32[]{:S(2)}) collective-permute-start(f32[64,256]{1,0:T(8,128)S(1)} %get-tuple-element.75), channel_id=1, source_target_pairs={{0,1},{1,2},{2,3},{3,4},{4,5},{5,6},{6,7},{7,8},{8,9},{9,10},{10,1... | collective-permute-start | bytes 196616 | tf_op jit(solution)/shard_map/ppermute | solution.py:73
  126.5 8.6 %second_inner.1.part_ref = f32[128,192]{1,0:T(8,128)S(1)} custom-call(s32[16,3]{1,0:T(8,128)S(1)} %broadcast_subtract_fusion.col_ref, f32[128,2048]{1,0:T(8,128)S(1)} %mix_pair.1.xp_ref.refs_3_, f32[64,2048]{1,0:T(8,128)S(1)} %get-tuple-element.54.s_ref.refs_4_, f32[16,3,128,128]{3,2,1,0:T(8,128)S(1)} %copy-done, f32[16,3,128,128]{3,2,1,0:T(8,128)} %m_ref.11, ...), custom_call_target="tpu_custom_call" | custom-call | flops 2415919104 | bytes 6291456 | tf_op jit(solution)/shard_map/second_inner/pallas_call | solution.py:558
  135.2 3.7 %second_edges.1 = f32[192,128]{1,0:T(8,128)S(1)} custom-call(s32[16,3]{1,0:T(8,128)S(1)} %broadcast_subtract_fusion.col_ref, f32[128,2048]{1,0:T(8,128)S(1)} %mix_pair.1.xp_ref.refs_3_, f32[64,2048]{1,0:T(8,128)S(1)} %get-tuple-element.54.s_ref.refs_4_, f32[64,256]{1,0:T(8,128)S(1)} %collective-permute-done.18.low_ref, ...), custom_call_target="tpu_custom_call" | custom-call | tf_op jit(solution)/shard_map/second_edges/pallas_call | solution.py:563
  138.9 1.3 collective-permute-done.20
  140.2 2.1 %collective-permute-start.23 = (f32[192,128]{1,0:T(8,128)S(1)}, f32[192,128]{1,0:T(8,128)S(1)}, u32[]{:S(2)}, u32[]{:S(2)}) collective-permute-start(f32[192,128]{1,0:T(8,128)S(1)} %add.82), channel_id=1, source_target_pairs={{0,48},{1,49},{2,50},{3,51},{4,52},{5,53},{6,54},{7,55},{8,56},{9,... | collective-permute-start | bytes 294920 | tf_op jit(solution)/shard_map/ppermute | solution.py:36
  142.4 2.1 %collective-permute-start.22 = (f32[192,128]{1,0:T(8,128)S(1)}, f32[192,128]{1,0:T(8,128)S(1)}, u32[]{:S(2)}, u32[]{:S(2)}) collective-permute-start(f32[192,128]{1,0:T(8,128)S(1)} %add.82), channel_id=1, source_target_pairs={{0,32},{1,33},{2,34},{3,35},{4,36},{5,37},{6,38},{7,39},{8,40},{9,... | collective-permute-start | bytes 294920 | tf_op jit(solution)/shard_map/ppermute | solution.py:36
  144.5 0.3 collective-permute-start.21
  144.7 1.3 collective-permute-done.23
  146.1 3.4 %collective-permute-done.22 = f32[192,128]{1,0:T(8,128)S(1)} collective-permute-done((f32[192,128]{1,0:T(8,128)S(1)}, f32[192,128]{1,0:T(8,128)S(1)}, u32[]{:S(2)}, u32[]{:S(2)}) %collective-permute-start.22) | collective-permute-done | bytes 98336 | tf_op jit(solution)/shard_map/ppermute | solution.py:36
  149.5 0.2 collective-permute-done.21
  149.8 1.7 collective-permute-start.26
  151.5 0.8 collective-permute-start.25
  152.3 1.7 collective-permute-start.24
  153.9 2.9 %collective-permute-done.26 = f32[192,128]{1,0:T(8,128)S(1)} collective-permute-done((f32[192,128]{1,0:T(8,128)S(1)}, f32[192,128]{1,0:T(8,128)S(1)}, u32[]{:S(2)}, u32[]{:S(2)}) %collective-permute-start.26) | collective-permute-done | bytes 98336 | tf_op jit(solution)/shard_map/ppermute | solution.py:36
  156.8 1.0 collective-permute-done.25
  157.9 2.0 %collective-permute-start.29 = (f32[192,128]{1,0:T(8,128)S(1)}, f32[192,128]{1,0:T(8,128)S(1)}, u32[]{:S(2)}, u32[]{:S(2)}) collective-permute-start(f32[192,128]{1,0:T(8,128)S(1)} %add_add_fusion.1), channel_id=1, source_target_pairs={{0,192},{1,193},{2,194},{3,195},{4,196},{5,197},{6,198},{7,199},{8... | collective-permute-start | bytes 294920 | tf_op jit(solution)/shard_map/ppermute | solution.py:36
  159.9 0.6 collective-permute-start.28
  160.5 1.8 collective-permute-start.27
  162.3 3.0 %next_first.1 = (f32[192,128]{1,0:T(8,128)S(1)}, f32[64,64]{1,0:T(8,128)S(1)}) custom-call(f32[192,128]{1,0:T(8,128)S(1)} %get-tuple-element.59.first_ref, f32[192,128]{1,0:T(8,128)S(1)} %get-tuple-element.60.second_ref, f32[192,128]{1,0:T(8,128)S(1)} %get-tuple-element.61.pair_ref), custom_call_target="tpu_custom_call" | custom-call | tf_op jit(solution)/shard_map/next_first/pallas_call | solution.py:552
  165.3 2.5 %collective-permute-done.28 = f32[192,128]{1,0:T(8,128)S(1)} collective-permute-done((f32[192,128]{1,0:T(8,128)S(1)}, f32[192,128]{1,0:T(8,128)S(1)}, u32[]{:S(2)}, u32[]{:S(2)}) %collective-permute-start.28) | collective-permute-done | bytes 98336 | tf_op jit(solution)/shard_map/ppermute | solution.py:36
  167.9 1.7 collective-permute-start.30
  169.6 2.7 %factor_pair.1.refs_2_ = f32[320,64]{1,0:T(8,128)S(1)} custom-call(f32[192,128]{1,0:T(8,128)S(1)} %get-tuple-element.67.first_ref.refs_0_, f32[64,64]{1,0:T(8,128)S(1)} %get-tuple-element.66.inv_ref), custom_call_target="tpu_custom_call" | custom-call | tf_op jit(solution)/shard_map/factor_pair/pallas_call | solution.py:549
  172.3 4.9 %collective-permute-done.30 = f32[192,128]{1,0:T(8,128)S(1)} collective-permute-done((f32[192,128]{1,0:T(8,128)S(1)}, f32[192,128]{1,0:T(8,128)S(1)}, u32[]{:S(2)}, u32[]{:S(2)}) %collective-permute-start.30) | collective-permute-done | bytes 98336 | tf_op jit(solution)/shard_map/ppermute | solution.py:36
  177.3 8.4 %last_mix.1 = (f32[64,2048]{1,0:T(8,128)}, f32[64,2048]{1,0:T(8,128)}) custom-call(f32[192,128]{1,0:T(8,128)S(1)} %get-tuple-element.67.first_ref.refs_0_, f32[192,128]{1,0:T(8,128)S(1)} %add.92.refs_1_, f32[320,64]{1,0:T(8,128)S(1)} %factor_pair.1.refs_2_, f32[128,2048]{1,0:T(8,128)S(1)} %mix_pair.1.xp_ref.refs_3_, ...), custom_call_target="tpu_custom_call" | custom-call | tf_op jit(solution)/shard_map/last_mix/pallas_call | solution.py:571
  (34 shorter events, 0.8 us)
Async XLA Ops:
  2.8 21.6 %collective-permute-start.1 = (f32[128,256]{1,0:T(8,128)S(1)}, f32[128,256]{1,0:T(8,128)S(1)}, u32[]{:S(2)}, u32[]{:S(2)}) collective-permute-start(f32[128,256]{1,0:T(8,128)S(1)} %get-tuple-element.72), channel_id=1, source_target_pairs={{1,0},{2,1},{3,2},{4,3},{5,4},{6,5},{7,6},{8,7},{9,8},{10,9},{11,1... | collective-permute-start | bytes 393224 | tf_op jit(solution)/shard_map/ppermute | solution.py:74
  13.8 15.6 %collective-permute-start = (f32[128,256]{1,0:T(8,128)S(1)}, f32[128,256]{1,0:T(8,128)S(1)}, u32[]{:S(2)}, u32[]{:S(2)}) collective-permute-start(f32[128,256]{1,0:T(8,128)S(1)} %get-tuple-element.73), channel_id=1, source_target_pairs={{0,1},{1,2},{2,3},{3,4},{4,5},{5,6},{6,7},{7,8},{8,9},{9,10},{10,1... | collective-permute-start | bytes 393224 | tf_op jit(solution)/shard_map/ppermute | solution.py:73
  16.5 0.7 copy-start.1
  17.2 0.7 copy-start.3
  32.2 16.7 %collective-permute-start.3 = (f32[128,256]{1,0:T(8,128)S(1)}, f32[128,256]{1,0:T(8,128)S(1)}, u32[]{:S(2)}, u32[]{:S(2)}) collective-permute-start(f32[128,256]{1,0:T(8,128)S(1)} %get-tuple-element.70), channel_id=1, source_target_pairs={{1,0},{2,1},{3,2},{4,3},{5,4},{6,5},{7,6},{8,7},{9,8},{10,9},{11,1... | collective-permute-start | bytes 393224 | tf_op jit(solution)/shard_map/ppermute | solution.py:74
  37.9 15.1 %collective-permute-start.2 = (f32[128,256]{1,0:T(8,128)S(1)}, f32[128,256]{1,0:T(8,128)S(1)}, u32[]{:S(2)}, u32[]{:S(2)}) collective-permute-start(f32[128,256]{1,0:T(8,128)S(1)} %get-tuple-element.71), channel_id=1, source_target_pairs={{0,1},{1,2},{2,3},{3,4},{4,5},{5,6},{6,7},{7,8},{8,9},{9,10},{10,1... | collective-permute-start | bytes 393224 | tf_op jit(solution)/shard_map/ppermute | solution.py:73
  53.0 48.1 %copy-start.2 = (f32[2048]{0:T(1024)S(1)}, f32[2048]{0:T(1024)}, u32[]{:S(2)}) copy-start(f32[2048]{0:T(1024)} %param.12) | copy-start | bytes 24580
  56.1 4.5 %collective-permute-start.4 = (f32[160,128]{1,0:T(8,128)S(1)}, f32[160,128]{1,0:T(8,128)S(1)}, u32[]{:S(2)}, u32[]{:S(2)}) collective-permute-start(f32[160,128]{1,0:T(8,128)S(1)} %get-tuple-element.46), channel_id=1, source_target_pairs={{0,16},{1,17},{2,18},{3,19},{4,20},{5,21},{6,22},{7,23},{8,24},{9,... | collective-permute-start | bytes 245768 | tf_op jit(solution)/shard_map/ppermute | solution.py:36
  56.2 6.2 %collective-permute-start.5 = (f32[160,128]{1,0:T(8,128)S(1)}, f32[160,128]{1,0:T(8,128)S(1)}, u32[]{:S(2)}, u32[]{:S(2)}) collective-permute-start(f32[160,128]{1,0:T(8,128)S(1)} %get-tuple-element.47), channel_id=1, source_target_pairs={{0,32},{1,33},{2,34},{3,35},{4,36},{5,37},{6,38},{7,39},{8,40},{9,... | collective-permute-start | bytes 245768 | tf_op jit(solution)/shard_map/ppermute | solution.py:36
  59.1 4.4 %collective-permute-start.6 = (f32[160,128]{1,0:T(8,128)S(1)}, f32[160,128]{1,0:T(8,128)S(1)}, u32[]{:S(2)}, u32[]{:S(2)}) collective-permute-start(f32[160,128]{1,0:T(8,128)S(1)} %get-tuple-element.48), channel_id=1, source_target_pairs={{0,48},{1,49},{2,50},{3,51},{4,52},{5,53},{6,54},{7,55},{8,56},{9,... | collective-permute-start | bytes 245768 | tf_op jit(solution)/shard_map/ppermute | solution.py:36
  63.6 1.4 collective-permute-start.7
  65.0 7.6 %collective-permute-start.10 = (f32[160,128]{1,0:T(8,128)S(1)}, f32[160,128]{1,0:T(8,128)S(1)}, u32[]{:S(2)}, u32[]{:S(2)}) collective-permute-start(f32[160,128]{1,0:T(8,128)S(1)} %add.74), channel_id=1, source_target_pairs={{0,12},{1,13},{2,14},{3,15},{4,8},{5,9},{6,10},{7,11},{8,4},{9,5},... | collective-permute-start | bytes 245768 | tf_op jit(solution)/shard_map/ppermute | solution.py:36
  65.4 7.1 %collective-permute-start.9 = (f32[160,128]{1,0:T(8,128)S(1)}, f32[160,128]{1,0:T(8,128)S(1)}, u32[]{:S(2)}, u32[]{:S(2)}) collective-permute-start(f32[160,128]{1,0:T(8,128)S(1)} %add.74), channel_id=1, source_target_pairs={{0,8},{1,9},{2,10},{3,11},{4,12},{5,13},{6,14},{7,15},{8,0},{9,1},... | collective-permute-start | bytes 245768 | tf_op jit(solution)/shard_map/ppermute | solution.py:36
  66.5 6.6 %collective-permute-start.8 = (f32[160,128]{1,0:T(8,128)S(1)}, f32[160,128]{1,0:T(8,128)S(1)}, u32[]{:S(2)}, u32[]{:S(2)}) collective-permute-start(f32[160,128]{1,0:T(8,128)S(1)} %add.74), channel_id=1, source_target_pairs={{0,4},{1,5},{2,6},{3,7},{4,0},{5,1},{6,2},{7,3},{8,12},{9,13},{10,... | collective-permute-start | bytes 245768 | tf_op jit(solution)/shard_map/ppermute | solution.py:36
  73.1 7.6 %collective-permute-start.13 = (f32[160,128]{1,0:T(8,128)S(1)}, f32[160,128]{1,0:T(8,128)S(1)}, u32[]{:S(2)}, u32[]{:S(2)}) collective-permute-start(f32[160,128]{1,0:T(8,128)S(1)} %add_add_fusion.4), channel_id=1, source_target_pairs={{0,192},{1,193},{2,194},{3,195},{4,196},{5,197},{6,198},{7,199},{8... | collective-permute-start | bytes 245768 | tf_op jit(solution)/shard_map/ppermute | solution.py:36
  77.9 6.2 %collective-permute-start.12 = (f32[160,128]{1,0:T(8,128)S(1)}, f32[160,128]{1,0:T(8,128)S(1)}, u32[]{:S(2)}, u32[]{:S(2)}) collective-permute-start(f32[160,128]{1,0:T(8,128)S(1)} %add_add_fusion.4), channel_id=1, source_target_pairs={{0,128},{1,129},{2,130},{3,131},{4,132},{5,133},{6,134},{7,135},{8... | collective-permute-start | bytes 245768 | tf_op jit(solution)/shard_map/ppermute | solution.py:36
  77.9 6.2 %collective-permute-start.11 = (f32[160,128]{1,0:T(8,128)S(1)}, f32[160,128]{1,0:T(8,128)S(1)}, u32[]{:S(2)}, u32[]{:S(2)}) collective-permute-start(f32[160,128]{1,0:T(8,128)S(1)} %add_add_fusion.4), channel_id=1, source_target_pairs={{0,64},{1,65},{2,66},{3,67},{4,68},{5,69},{6,70},{7,71},{8,72},{9,... | collective-permute-start | bytes 245768 | tf_op jit(solution)/shard_map/ppermute | solution.py:36
  84.1 8.5 %collective-permute-start.14 = (f32[160,128]{1,0:T(8,128)S(1)}, f32[160,128]{1,0:T(8,128)S(1)}, u32[]{:S(2)}, u32[]{:S(2)}) collective-permute-start(f32[160,128]{1,0:T(8,128)S(1)} %add_add_fusion.3), channel_id=1, source_target_pairs={{0,1},{1,0},{2,3},{3,2},{4,5},{5,4},{6,7},{7,6},{8,9},{9,8},{10,11... | collective-permute-start | bytes 245768 | tf_op jit(solution)/shard_map/ppermute | solution.py:36
  92.7 4.9 %collective-permute-start.17 = (f32[160,128]{1,0:T(8,128)S(1)}, f32[160,128]{1,0:T(8,128)S(1)}, u32[]{:S(2)}, u32[]{:S(2)}) collective-permute-start(f32[160,128]{1,0:T(8,128)S(1)} %add.81.refs_1_), channel_id=1, source_target_pairs={{0,48},{1,49},{2,50},{3,51},{4,52},{5,53},{6,54},{7,55},{8,56},{9,... | collective-permute-start | bytes 245768 | tf_op jit(solution)/shard_map/ppermute | solution.py:36
  93.0 6.4 %collective-permute-start.16 = (f32[160,128]{1,0:T(8,128)S(1)}, f32[160,128]{1,0:T(8,128)S(1)}, u32[]{:S(2)}, u32[]{:S(2)}) collective-permute-start(f32[160,128]{1,0:T(8,128)S(1)} %add.81.refs_1_), channel_id=1, source_target_pairs={{0,32},{1,33},{2,34},{3,35},{4,36},{5,37},{6,38},{7,39},{8,40},{9,... | collective-permute-start | bytes 245768 | tf_op jit(solution)/shard_map/ppermute | solution.py:36
  96.7 4.4 %collective-permute-start.15 = (f32[160,128]{1,0:T(8,128)S(1)}, f32[160,128]{1,0:T(8,128)S(1)}, u32[]{:S(2)}, u32[]{:S(2)}) collective-permute-start(f32[160,128]{1,0:T(8,128)S(1)} %add.81.refs_1_), channel_id=1, source_target_pairs={{0,16},{1,17},{2,18},{3,19},{4,20},{5,21},{6,22},{7,23},{8,24},{9,... | collective-permute-start | bytes 245768 | tf_op jit(solution)/shard_map/ppermute | solution.py:36
  101.2 25.3 %copy-start = (f32[16,3,128,128]{3,2,1,0:T(8,128)S(1)}, f32[16,3,128,128]{3,2,1,0:T(8,128)}, u32[]{:S(2)}) copy-start(f32[16,3,128,128]{3,2,1,0:T(8,128)} %k_ref.11) | copy-start | bytes 9437188
  116.7 18.4 %collective-permute-start.19 = (f32[64,256]{1,0:T(8,128)S(1)}, f32[64,256]{1,0:T(8,128)S(1)}, u32[]{:S(2)}, u32[]{:S(2)}) collective-permute-start(f32[64,256]{1,0:T(8,128)S(1)} %get-tuple-element.74), channel_id=1, source_target_pairs={{1,0},{2,1},{3,2},{4,3},{5,4},{6,5},{7,6},{8,7},{9,8},{10,9},{11,1... | collective-permute-start | bytes 196616 | tf_op jit(solution)/shard_map/ppermute | solution.py:74
  119.0 16.2 %collective-permute-start.18 = (f32[64,256]{1,0:T(8,128)S(1)}, f32[64,256]{1,0:T(8,128)S(1)}, u32[]{:S(2)}, u32[]{:S(2)}) collective-permute-start(f32[64,256]{1,0:T(8,128)S(1)} %get-tuple-element.75), channel_id=1, source_target_pairs={{0,1},{1,2},{2,3},{3,4},{4,5},{5,6},{6,7},{7,8},{8,9},{9,10},{10,1... | collective-permute-start | bytes 196616 | tf_op jit(solution)/shard_map/ppermute | solution.py:73
  138.8 1.4 collective-permute-start.20
  140.2 5.8 %collective-permute-start.23 = (f32[192,128]{1,0:T(8,128)S(1)}, f32[192,128]{1,0:T(8,128)S(1)}, u32[]{:S(2)}, u32[]{:S(2)}) collective-permute-start(f32[192,128]{1,0:T(8,128)S(1)} %add.82), channel_id=1, source_target_pairs={{0,48},{1,49},{2,50},{3,51},{4,52},{5,53},{6,54},{7,55},{8,56},{9,... | collective-permute-start | bytes 294920 | tf_op jit(solution)/shard_map/ppermute | solution.py:36
  142.4 7.1 %collective-permute-start.22 = (f32[192,128]{1,0:T(8,128)S(1)}, f32[192,128]{1,0:T(8,128)S(1)}, u32[]{:S(2)}, u32[]{:S(2)}) collective-permute-start(f32[192,128]{1,0:T(8,128)S(1)} %add.82), channel_id=1, source_target_pairs={{0,32},{1,33},{2,34},{3,35},{4,36},{5,37},{6,38},{7,39},{8,40},{9,... | collective-permute-start | bytes 294920 | tf_op jit(solution)/shard_map/ppermute | solution.py:36
  144.5 5.2 %collective-permute-start.21 = (f32[192,128]{1,0:T(8,128)S(1)}, f32[192,128]{1,0:T(8,128)S(1)}, u32[]{:S(2)}, u32[]{:S(2)}) collective-permute-start(f32[192,128]{1,0:T(8,128)S(1)} %add.82), channel_id=1, source_target_pairs={{0,16},{1,17},{2,18},{3,19},{4,20},{5,21},{6,22},{7,23},{8,24},{9,... | collective-permute-start | bytes 294920 | tf_op jit(solution)/shard_map/ppermute | solution.py:36
  149.8 7.1 %collective-permute-start.26 = (f32[192,128]{1,0:T(8,128)S(1)}, f32[192,128]{1,0:T(8,128)S(1)}, u32[]{:S(2)}, u32[]{:S(2)}) collective-permute-start(f32[192,128]{1,0:T(8,128)S(1)} %add_add_fusion.2), channel_id=1, source_target_pairs={{0,12},{1,13},{2,14},{3,15},{4,8},{5,9},{6,10},{7,11},{8,4},{9,5},... | collective-permute-start | bytes 294920 | tf_op jit(solution)/shard_map/ppermute | solution.py:36
  151.5 6.3 %collective-permute-start.25 = (f32[192,128]{1,0:T(8,128)S(1)}, f32[192,128]{1,0:T(8,128)S(1)}, u32[]{:S(2)}, u32[]{:S(2)}) collective-permute-start(f32[192,128]{1,0:T(8,128)S(1)} %add_add_fusion.2), channel_id=1, source_target_pairs={{0,8},{1,9},{2,10},{3,11},{4,12},{5,13},{6,14},{7,15},{8,0},{9,1},... | collective-permute-start | bytes 294920 | tf_op jit(solution)/shard_map/ppermute | solution.py:36
  152.3 5.6 %collective-permute-start.24 = (f32[192,128]{1,0:T(8,128)S(1)}, f32[192,128]{1,0:T(8,128)S(1)}, u32[]{:S(2)}, u32[]{:S(2)}) collective-permute-start(f32[192,128]{1,0:T(8,128)S(1)} %add_add_fusion.2), channel_id=1, source_target_pairs={{0,4},{1,5},{2,6},{3,7},{4,0},{5,1},{6,2},{7,3},{8,12},{9,13},{10,... | collective-permute-start | bytes 294920 | tf_op jit(solution)/shard_map/ppermute | solution.py:36
  157.9 7.5 %collective-permute-start.29 = (f32[192,128]{1,0:T(8,128)S(1)}, f32[192,128]{1,0:T(8,128)S(1)}, u32[]{:S(2)}, u32[]{:S(2)}) collective-permute-start(f32[192,128]{1,0:T(8,128)S(1)} %add_add_fusion.1), channel_id=1, source_target_pairs={{0,192},{1,193},{2,194},{3,195},{4,196},{5,197},{6,198},{7,199},{8... | collective-permute-start | bytes 294920 | tf_op jit(solution)/shard_map/ppermute | solution.py:36
  159.9 7.9 %collective-permute-start.28 = (f32[192,128]{1,0:T(8,128)S(1)}, f32[192,128]{1,0:T(8,128)S(1)}, u32[]{:S(2)}, u32[]{:S(2)}) collective-permute-start(f32[192,128]{1,0:T(8,128)S(1)} %add_add_fusion.1), channel_id=1, source_target_pairs={{0,128},{1,129},{2,130},{3,131},{4,132},{5,133},{6,134},{7,135},{8... | collective-permute-start | bytes 294920 | tf_op jit(solution)/shard_map/ppermute | solution.py:36
  160.5 7.3 %collective-permute-start.27 = (f32[192,128]{1,0:T(8,128)S(1)}, f32[192,128]{1,0:T(8,128)S(1)}, u32[]{:S(2)}, u32[]{:S(2)}) collective-permute-start(f32[192,128]{1,0:T(8,128)S(1)} %add_add_fusion.1), channel_id=1, source_target_pairs={{0,64},{1,65},{2,66},{3,67},{4,68},{5,69},{6,70},{7,71},{8,72},{9,... | collective-permute-start | bytes 294920 | tf_op jit(solution)/shard_map/ppermute | solution.py:36
  167.9 9.4 %collective-permute-start.30 = (f32[192,128]{1,0:T(8,128)S(1)}, f32[192,128]{1,0:T(8,128)S(1)}, u32[]{:S(2)}, u32[]{:S(2)}) collective-permute-start(f32[192,128]{1,0:T(8,128)S(1)} %add_add_fusion), channel_id=1, source_target_pairs={{0,1},{1,0},{2,3},{3,2},{4,5},{5,4},{6,7},{7,6},{8,9},{9,8},{10,11... | collective-permute-start | bytes 294920 | tf_op jit(solution)/shard_map/ppermute | solution.py:36

commit v2 on v1

--- a/solution.py
+++ b/solution.py
@@ -83,7 +83,10 @@
     def dot(u, v):
         return lax.dot_general(u, v, (dims, ((), ())), preferred_element_type=jnp.float32)
 
-    return dot(a[0], b[0]) + (dot(a[0], b[1]) + dot(a[1], b[0]))
+    kept = 1 - dims[0][0]
+    size = a[0].shape[kept]
+    stacked = dot(jnp.concatenate(a, kept), b[0])
+    return stacked[:size] + (dot(a[0], b[1]) + stacked[size:])
 
 
 NT = ((1,), (1,))

time: 186 us -> 184 us (0.989)
  Pallas kernels: 61.3 us -> 58.6 us
  transfers between devices with their start and end apart: 31 -> 31, of which waited for: 22 -> 21; matrix products, arithmetic and copies ran while one was open for 0% -> 0% of each run, Pallas kernels for 15% -> 14%
where the time goes in v2:
time: 184 us; the launch traced here: 183 us
  starting transfers between devices  65.2 us (35%)
  Pallas kernels  58.6 us (32%)
  waiting for transfers between devices  53.5 us (29%)
  local copies, waits for them, and re-layouts  4.37 us (2%)
    ppermute x25, waiting for transfers between devices, partner(): return lax.ppermute(x, AXES, pairs)  44.4 us
    ppermute x25, starting transfers between devices, partner(): return lax.ppermute(x, AXES, pairs)  32.8 us
    ppermute x3, starting transfers between devices, exchange(): lax.ppermute(head, AXES, [(i + 1, i) for i in range(count - 1)])  19 us
    pallas_call x1, Pallas kernels, shards(): call(lambda *refs: second_search(total_rows, *refs), 'second_search', [sm...  14.5 us
    ppermute x3, starting transfers between devices, exchange(): low = lax.ppermute(tail, AXES, [(i, i + 1) for i in range(count - 1)])  13.4 us
    ppermute x3, waiting for transfers between devices, exchange(): low = lax.ppermute(tail, AXES, [(i, i + 1) for i in range(count - 1)])  9.04 us
    pallas_call x1, Pallas kernels, shards(): call(lambda *refs: last_kernel(total_rows, *refs), 'last_mix', [whole()]...  8.35 us
    pallas_call x1, Pallas kernels, shards(): call(search_inner, 'second_inner', [smem()] + [whole()] * 2 + stored(insi...  6.93 us
  transfers between devices with their start and end apart: 31, of which 21 were waited for; matrix products, arithmetic and copies ran while one was open for 0% of the time, Pallas kernels for 14%

profile of v2, /device:TPU:2, one launch (start us, length us, event | category | flops | bytes accessed | tf_op | source)
XLA Modules:
  0.0 182.7 jit_solution(8810890526360826796)
XLA Ops:
  0.6 1.1 constant_dynamic-update-slice_fusion.1
  1.7 1.1 constant_dynamic-update-slice_fusion.xp_ref
  2.8 11.0 %collective-permute-start.1 = (f32[128,256]{1,0:T(8,128)S(1)}, f32[128,256]{1,0:T(8,128)S(1)}, u32[]{:S(2)}, u32[]{:S(2)}) collective-permute-start(f32[128,256]{1,0:T(8,128)S(1)} %get-tuple-element.72), channel_id=1, source_target_pairs={{1,0},{2,1},{3,2},{4,3},{5,4},{6,5},{7,6},{8,7},{9,8},{10,9},{11,1... | collective-permute-start | bytes 393224 | tf_op jit(solution)/shard_map/ppermute | solution.py:74
  13.8 1.9 %collective-permute-start = (f32[128,256]{1,0:T(8,128)S(1)}, f32[128,256]{1,0:T(8,128)S(1)}, u32[]{:S(2)}, u32[]{:S(2)}) collective-permute-start(f32[128,256]{1,0:T(8,128)S(1)} %get-tuple-element.73), channel_id=1, source_target_pairs={{0,1},{1,2},{2,3},{3,4},{4,5},{5,6},{6,7},{7,8},{8,9},{9,10},{10,1... | collective-permute-start | bytes 393224 | tf_op jit(solution)/shard_map/ppermute | solution.py:73
  15.7 0.8 copy.14
  16.5 0.7 copy-done.1
  17.2 0.7 copy-done.3
  17.9 6.5 %pair_inner.1 = (f32[128,2048]{1,0:T(8,128)S(1)}, f32[128,2048]{1,0:T(8,128)S(1)}, f32[128,2048]{1,0:T(8,128)S(1)}, f32[256,128]{1,0:T(8,128)S(1)}) custom-call(s32[16,3]{1,0:T(8,128)S(1)} %broadcast_subtract_fusion.col_ref, f32[128,2048]{1,0:T(8,128)S(1)} %constant_dynamic-update-slice_fusion.xp_ref, f32[16,3,128,128]{3,2,1,0:T(8,128)} %k_ref.11, ...), custom_call_target="tpu_custom_call" | custom-call | flops 2415919104 | bytes 6291456 | tf_op jit(solution)/shard_map/pair_inner/pallas_call | solution.py:509
  24.4 4.9 %collective-permute-done.low_ref = f32[128,256]{1,0:T(8,128)S(1)} collective-permute-done((f32[128,256]{1,0:T(8,128)S(1)}, f32[128,256]{1,0:T(8,128)S(1)}, u32[]{:S(2)}, u32[]{:S(2)}) %collective-permute-start) | collective-permute-done | bytes 131104 | tf_op jit(solution)/shard_map/ppermute | solution.py:73
  29.4 2.8 %pair_edges.1 = (f32[128,2048]{1,0:T(8,128)S(1)}, f32[128,2048]{1,0:T(8,128)S(1)}, f32[128,2048]{1,0:T(8,128)S(1)}, f32[192,128]{1,0:T(8,128)S(1)}) custom-call(s32[16,3]{1,0:T(8,128)S(1)} %broadcast_subtract_fusion.col_ref, f32[128,2048]{1,0:T(8,128)S(1)} %constant_dynamic-update-slice_fusion.xp_ref, ...), custom_call_target="tpu_custom_call", output_to_operand_aliasing={{0}: (5, {}), {1}: (6, {}), {2}: (7, {})} | custom-call | tf_op jit(solution)/shard_map/pair_edges/pallas_call | solution.py:516
  32.2 5.7 %collective-permute-start.3 = (f32[128,256]{1,0:T(8,128)S(1)}, f32[128,256]{1,0:T(8,128)S(1)}, u32[]{:S(2)}, u32[]{:S(2)}) collective-permute-start(f32[128,256]{1,0:T(8,128)S(1)} %get-tuple-element.70), channel_id=1, source_target_pairs={{1,0},{2,1},{3,2},{4,3},{5,4},{6,5},{7,6},{8,7},{9,8},{10,9},{11,1... | collective-permute-start | bytes 393224 | tf_op jit(solution)/shard_map/ppermute | solution.py:74
  37.9 4.1 %collective-permute-start.2 = (f32[128,256]{1,0:T(8,128)S(1)}, f32[128,256]{1,0:T(8,128)S(1)}, u32[]{:S(2)}, u32[]{:S(2)}) collective-permute-start(f32[128,256]{1,0:T(8,128)S(1)} %get-tuple-element.71), channel_id=1, source_target_pairs={{0,1},{1,2},{2,3},{3,4},{4,5},{5,6},{6,7},{7,8},{8,9},{9,10},{10,1... | collective-permute-start | bytes 393224 | tf_op jit(solution)/shard_map/ppermute | solution.py:73
  42.0 6.9 %parts_inner.1 = (f32[128,2048]{1,0:T(8,128)S(1)}, f32[128,2048]{1,0:T(8,128)S(1)}, f32[256,256]{1,0:T(8,128)S(1)}) custom-call(s32[16,3]{1,0:T(8,128)S(1)} %broadcast_subtract_fusion.col_ref, f32[128,2048]{1,0:T(8,128)S(1)} %constant_dynamic-update-slice_fusion.xp_ref, f32[128,2048]{1,0:T(8,128)S(1)} %get-tuple-element.40.parts_ref.s_ref, ...), custom_call_target="tpu_custom_call" | custom-call | flops 2415919104 | bytes 6291456 | tf_op jit(solution)/shard_map/parts_inner/pallas_call | solution.py:525
  48.9 4.1 %collective-permute-done.2.low_ref = f32[128,256]{1,0:T(8,128)S(1)} collective-permute-done((f32[128,256]{1,0:T(8,128)S(1)}, f32[128,256]{1,0:T(8,128)S(1)}, u32[]{:S(2)}, u32[]{:S(2)}) %collective-permute-start.2) | collective-permute-done | bytes 131104 | tf_op jit(solution)/shard_map/ppermute | solution.py:73
  53.0 3.0 %parts_edges.1 = (f32[128,2048]{1,0:T(8,128)S(1)}, f32[128,2048]{1,0:T(8,128)S(1)}, f32[160,128]{1,0:T(8,128)S(1)}, f32[160,128]{1,0:T(8,128)S(1)}, f32[160,128]{1,0:T(8,128)S(1)}, /*index=5*/f32[160,128]{1,0:T(8,128)S(1)}) custom-call(s32[16,3]{1,0:T(8,128)S(1)} %broadcast_subtract_fusion.col_ref, ...), custom_call_target="tpu_custom_call", output_to_operand_aliasing={{0}: (8, {}), {1}: (9, {})} | custom-call | tf_op jit(solution)/shard_map/parts_edges/pallas_call | solution.py:533
  56.1 0.1 collective-permute-start.4
  56.2 2.9 %collective-permute-start.5 = (f32[160,128]{1,0:T(8,128)S(1)}, f32[160,128]{1,0:T(8,128)S(1)}, u32[]{:S(2)}, u32[]{:S(2)}) collective-permute-start(f32[160,128]{1,0:T(8,128)S(1)} %get-tuple-element.47), channel_id=1, source_target_pairs={{0,32},{1,33},{2,34},{3,35},{4,36},{5,37},{6,38},{7,39},{8,40},{9,... | collective-permute-start | bytes 245768 | tf_op jit(solution)/shard_map/ppermute | solution.py:36
  59.1 0.5 collective-permute-start.6
  59.6 1.0 collective-permute-done.4
  60.6 1.8 collective-permute-done.5
  62.4 1.1 collective-permute-done.6
  63.7 1.3 collective-permute-done.7
  65.0 0.5 collective-permute-start.10
  65.4 1.1 collective-permute-start.9
  66.5 2.6 %collective-permute-start.8 = (f32[160,128]{1,0:T(8,128)S(1)}, f32[160,128]{1,0:T(8,128)S(1)}, u32[]{:S(2)}, u32[]{:S(2)}) collective-permute-start(f32[160,128]{1,0:T(8,128)S(1)} %add.74), channel_id=1, source_target_pairs={{0,4},{1,5},{2,6},{3,7},{4,0},{5,1},{6,2},{7,3},{8,12},{9,13},{10,... | collective-permute-start | bytes 245768 | tf_op jit(solution)/shard_map/ppermute | solution.py:36
  69.1 3.4 %collective-permute-done.10 = f32[160,128]{1,0:T(8,128)S(1)} collective-permute-done((f32[160,128]{1,0:T(8,128)S(1)}, f32[160,128]{1,0:T(8,128)S(1)}, u32[]{:S(2)}, u32[]{:S(2)}) %collective-permute-start.10) | collective-permute-done | bytes 81952 | tf_op jit(solution)/shard_map/ppermute | solution.py:36
  72.5 0.6 collective-permute-done.8
  73.1 4.8 %collective-permute-start.13 = (f32[160,128]{1,0:T(8,128)S(1)}, f32[160,128]{1,0:T(8,128)S(1)}, u32[]{:S(2)}, u32[]{:S(2)}) collective-permute-start(f32[160,128]{1,0:T(8,128)S(1)} %add_add_fusion.4), channel_id=1, source_target_pairs={{0,192},{1,193},{2,194},{3,195},{4,196},{5,197},{6,198},{7,199},{8... | collective-permute-start | bytes 245768 | tf_op jit(solution)/shard_map/ppermute | solution.py:36
  77.9 0.7 collective-permute-start.11
  78.6 2.1 %collective-permute-done.13 = f32[160,128]{1,0:T(8,128)S(1)} collective-permute-done((f32[160,128]{1,0:T(8,128)S(1)}, f32[160,128]{1,0:T(8,128)S(1)}, u32[]{:S(2)}, u32[]{:S(2)}) %collective-permute-start.13) | collective-permute-done | bytes 81952 | tf_op jit(solution)/shard_map/ppermute | solution.py:36
  80.7 3.4 %collective-permute-done.12 = f32[160,128]{1,0:T(8,128)S(1)} collective-permute-done((f32[160,128]{1,0:T(8,128)S(1)}, f32[160,128]{1,0:T(8,128)S(1)}, u32[]{:S(2)}, u32[]{:S(2)}) %collective-permute-start.12) | collective-permute-done | bytes 81952 | tf_op jit(solution)/shard_map/ppermute | solution.py:36
  84.2 0.2 collective-permute-start.14
  84.3 8.3 %collective-permute-done.14 = f32[160,128]{1,0:T(8,128)S(1)} collective-permute-done((f32[160,128]{1,0:T(8,128)S(1)}, f32[160,128]{1,0:T(8,128)S(1)}, u32[]{:S(2)}, u32[]{:S(2)}) %collective-permute-start.14) | collective-permute-done | bytes 81952 | tf_op jit(solution)/shard_map/ppermute | solution.py:36
  92.7 0.3 collective-permute-start.17
  93.0 3.6 %collective-permute-start.16 = (f32[160,128]{1,0:T(8,128)S(1)}, f32[160,128]{1,0:T(8,128)S(1)}, u32[]{:S(2)}, u32[]{:S(2)}) collective-permute-start(f32[160,128]{1,0:T(8,128)S(1)} %add.81.refs_1_), channel_id=1, source_target_pairs={{0,32},{1,33},{2,34},{3,35},{4,36},{5,37},{6,38},{7,39},{8,40},{9,... | collective-permute-start | bytes 245768 | tf_op jit(solution)/shard_map/ppermute | solution.py:36
  96.7 0.6 collective-permute-start.15
  97.3 0.3 collective-permute-done.17.refs_4_
  97.6 1.8 collective-permute-done.16.refs_3_
  99.4 1.8 collective-permute-done.15.refs_2_
  101.1 14.5 %second_search.1 = (f32[64,2048]{1,0:T(8,128)S(1)}, f32[192,128]{1,0:T(8,128)S(1)}, f32[256,128]{1,0:T(8,128)S(1)}, f32[192,128]{1,0:T(8,128)S(1)}, f32[192,128]{1,0:T(8,128)S(1)}) custom-call(s32[1]{0:T(128)} %bitcast.at_ref.refs_0_, f32[160,128]{1,0:T(8,128)S(1)} %add.81.refs_1_, f32[160,128]{1,0:T(8,128)S(1)} %collective-permute-done.15.refs_2_, ...), custom_call_target="tpu_custom_call" | custom-call | tf_op jit(solution)/shard_map/second_search/pallas_call | solution.py:544
  115.6 0.7 mix_pair.1.xp_ref.refs_3_
  116.4 2.4 %collective-permute-start.19 = (f32[64,256]{1,0:T(8,128)S(1)}, f32[64,256]{1,0:T(8,128)S(1)}, u32[]{:S(2)}, u32[]{:S(2)}) collective-permute-start(f32[64,256]{1,0:T(8,128)S(1)} %get-tuple-element.74), channel_id=1, source_target_pairs={{1,0},{2,1},{3,2},{4,3},{5,4},{6,5},{7,6},{8,7},{9,8},{10,9},{11,1... | collective-permute-start | bytes 196616 | tf_op jit(solution)/shard_map/ppermute | solution.py:74
  118.7 7.4 %collective-permute-start.18 = (f32[64,256]{1,0:T(8,128)S(1)}, f32[64,256]{1,0:T(8,128)S(1)}, u32[]{:S(2)}, u32[]{:S(2)}) collective-permute-start(f32[64,256]{1,0:T(8,128)S(1)} %get-tuple-element.75), channel_id=1, source_target_pairs={{0,1},{1,2},{2,3},{3,4},{4,5},{5,6},{6,7},{7,8},{8,9},{9,10},{10,1... | collective-permute-start | bytes 196616 | tf_op jit(solution)/shard_map/ppermute | solution.py:73
  126.1 6.9 %second_inner.1.part_ref = f32[128,192]{1,0:T(8,128)S(1)} custom-call(s32[16,3]{1,0:T(8,128)S(1)} %broadcast_subtract_fusion.col_ref, f32[128,2048]{1,0:T(8,128)S(1)} %mix_pair.1.xp_ref.refs_3_, f32[64,2048]{1,0:T(8,128)S(1)} %get-tuple-element.54.s_ref.refs_4_, f32[16,3,128,128]{3,2,1,0:T(8,128)S(1)} %copy-done, f32[16,3,128,128]{3,2,1,0:T(8,128)} %m_ref.11, ...), custom_call_target="tpu_custom_call" | custom-call | flops 2415919104 | bytes 6291456 | tf_op jit(solution)/shard_map/second_inner/pallas_call | solution.py:561
  133.1 3.1 %second_edges.1 = f32[192,128]{1,0:T(8,128)S(1)} custom-call(s32[16,3]{1,0:T(8,128)S(1)} %broadcast_subtract_fusion.col_ref, f32[128,2048]{1,0:T(8,128)S(1)} %mix_pair.1.xp_ref.refs_3_, f32[64,2048]{1,0:T(8,128)S(1)} %get-tuple-element.54.s_ref.refs_4_, f32[64,256]{1,0:T(8,128)S(1)} %collective-permute-done.18.low_ref, ...), custom_call_target="tpu_custom_call" | custom-call | tf_op jit(solution)/shard_map/second_edges/pallas_call | solution.py:566
  136.3 1.3 collective-permute-done.20
  137.6 2.1 %collective-permute-start.23 = (f32[192,128]{1,0:T(8,128)S(1)}, f32[192,128]{1,0:T(8,128)S(1)}, u32[]{:S(2)}, u32[]{:S(2)}) collective-permute-start(f32[192,128]{1,0:T(8,128)S(1)} %add.82), channel_id=1, source_target_pairs={{0,48},{1,49},{2,50},{3,51},{4,52},{5,53},{6,54},{7,55},{8,56},{9,... | collective-permute-start | bytes 294920 | tf_op jit(solution)/shard_map/ppermute | solution.py:36
  139.7 2.1 %collective-permute-start.22 = (f32[192,128]{1,0:T(8,128)S(1)}, f32[192,128]{1,0:T(8,128)S(1)}, u32[]{:S(2)}, u32[]{:S(2)}) collective-permute-start(f32[192,128]{1,0:T(8,128)S(1)} %add.82), channel_id=1, source_target_pairs={{0,32},{1,33},{2,34},{3,35},{4,36},{5,37},{6,38},{7,39},{8,40},{9,... | collective-permute-start | bytes 294920 | tf_op jit(solution)/shard_map/ppermute | solution.py:36
  141.9 1.9 %collective-permute-done.23 = f32[192,128]{1,0:T(8,128)S(1)} collective-permute-done((f32[192,128]{1,0:T(8,128)S(1)}, f32[192,128]{1,0:T(8,128)S(1)}, u32[]{:S(2)}, u32[]{:S(2)}) %collective-permute-start.23) | collective-permute-done | bytes 98336 | tf_op jit(solution)/shard_map/ppermute | solution.py:36
  143.8 3.1 %collective-permute-done.22 = f32[192,128]{1,0:T(8,128)S(1)} collective-permute-done((f32[192,128]{1,0:T(8,128)S(1)}, f32[192,128]{1,0:T(8,128)S(1)}, u32[]{:S(2)}, u32[]{:S(2)}) %collective-permute-start.22) | collective-permute-done | bytes 98336 | tf_op jit(solution)/shard_map/ppermute | solution.py:36
  146.9 1.8 collective-permute-start.26
  148.7 0.7 collective-permute-start.25
  149.4 1.7 collective-permute-start.24
  151.1 2.8 %collective-permute-done.26 = f32[192,128]{1,0:T(8,128)S(1)} collective-permute-done((f32[192,128]{1,0:T(8,128)S(1)}, f32[192,128]{1,0:T(8,128)S(1)}, u32[]{:S(2)}, u32[]{:S(2)}) %collective-permute-start.26) | collective-permute-done | bytes 98336 | tf_op jit(solution)/shard_map/ppermute | solution.py:36
  153.9 1.2 collective-permute-done.25
  155.1 2.0 %collective-permute-start.29 = (f32[192,128]{1,0:T(8,128)S(1)}, f32[192,128]{1,0:T(8,128)S(1)}, u32[]{:S(2)}, u32[]{:S(2)}) collective-permute-start(f32[192,128]{1,0:T(8,128)S(1)} %add_add_fusion.1), channel_id=1, source_target_pairs={{0,192},{1,193},{2,194},{3,195},{4,196},{5,197},{6,198},{7,199},{8... | collective-permute-start | bytes 294920 | tf_op jit(solution)/shard_map/ppermute | solution.py:36
  157.1 0.6 collective-permute-start.28
  157.7 1.9 %collective-permute-start.27 = (f32[192,128]{1,0:T(8,128)S(1)}, f32[192,128]{1,0:T(8,128)S(1)}, u32[]{:S(2)}, u32[]{:S(2)}) collective-permute-start(f32[192,128]{1,0:T(8,128)S(1)} %add_add_fusion.1), channel_id=1, source_target_pairs={{0,64},{1,65},{2,66},{3,67},{4,68},{5,69},{6,70},{7,71},{8,72},{9,... | collective-permute-start | bytes 294920 | tf_op jit(solution)/shard_map/ppermute | solution.py:36
  159.6 3.0 %next_first.1 = (f32[192,128]{1,0:T(8,128)S(1)}, f32[64,64]{1,0:T(8,128)S(1)}) custom-call(f32[192,128]{1,0:T(8,128)S(1)} %get-tuple-element.59.first_ref, f32[192,128]{1,0:T(8,128)S(1)} %get-tuple-element.60.second_ref, f32[192,128]{1,0:T(8,128)S(1)} %get-tuple-element.61.pair_ref), custom_call_target="tpu_custom_call" | custom-call | tf_op jit(solution)/shard_map/next_first/pallas_call | solution.py:555
  162.6 2.5 %collective-permute-done.28 = f32[192,128]{1,0:T(8,128)S(1)} collective-permute-done((f32[192,128]{1,0:T(8,128)S(1)}, f32[192,128]{1,0:T(8,128)S(1)}, u32[]{:S(2)}, u32[]{:S(2)}) %collective-permute-start.28) | collective-permute-done | bytes 98336 | tf_op jit(solution)/shard_map/ppermute | solution.py:36
  165.1 1.7 collective-permute-start.30
  166.8 2.7 %factor_pair.1.refs_2_ = f32[320,64]{1,0:T(8,128)S(1)} custom-call(f32[192,128]{1,0:T(8,128)S(1)} %get-tuple-element.67.first_ref.refs_0_, f32[64,64]{1,0:T(8,128)S(1)} %get-tuple-element.66.inv_ref), custom_call_target="tpu_custom_call" | custom-call | tf_op jit(solution)/shard_map/factor_pair/pallas_call | solution.py:552
  169.5 4.9 %collective-permute-done.30 = f32[192,128]{1,0:T(8,128)S(1)} collective-permute-done((f32[192,128]{1,0:T(8,128)S(1)}, f32[192,128]{1,0:T(8,128)S(1)}, u32[]{:S(2)}, u32[]{:S(2)}) %collective-permute-start.30) | collective-permute-done | bytes 98336 | tf_op jit(solution)/shard_map/ppermute | solution.py:36
  174.4 8.3 %last_mix.1 = (f32[64,2048]{1,0:T(8,128)}, f32[64,2048]{1,0:T(8,128)}) custom-call(f32[192,128]{1,0:T(8,128)S(1)} %get-tuple-element.67.first_ref.refs_0_, f32[192,128]{1,0:T(8,128)S(1)} %add.92.refs_1_, f32[320,64]{1,0:T(8,128)S(1)} %factor_pair.1.refs_2_, f32[128,2048]{1,0:T(8,128)S(1)} %mix_pair.1.xp_ref.refs_3_, ...), custom_call_target="tpu_custom_call" | custom-call | tf_op jit(solution)/shard_map/last_mix/pallas_call | solution.py:574
  (34 shorter events, 0.5 us)
Async XLA Ops:
  2.8 21.6 %collective-permute-start.1 = (f32[128,256]{1,0:T(8,128)S(1)}, f32[128,256]{1,0:T(8,128)S(1)}, u32[]{:S(2)}, u32[]{:S(2)}) collective-permute-start(f32[128,256]{1,0:T(8,128)S(1)} %get-tuple-element.72), channel_id=1, source_target_pairs={{1,0},{2,1},{3,2},{4,3},{5,4},{6,5},{7,6},{8,7},{9,8},{10,9},{11,1... | collective-permute-start | bytes 393224 | tf_op jit(solution)/shard_map/ppermute | solution.py:74
  13.8 15.6 %collective-permute-start = (f32[128,256]{1,0:T(8,128)S(1)}, f32[128,256]{1,0:T(8,128)S(1)}, u32[]{:S(2)}, u32[]{:S(2)}) collective-permute-start(f32[128,256]{1,0:T(8,128)S(1)} %get-tuple-element.73), channel_id=1, source_target_pairs={{0,1},{1,2},{2,3},{3,4},{4,5},{5,6},{6,7},{7,8},{8,9},{9,10},{10,1... | collective-permute-start | bytes 393224 | tf_op jit(solution)/shard_map/ppermute | solution.py:73
  16.5 0.7 copy-start.1
  17.2 0.7 copy-start.3
  32.2 16.7 %collective-permute-start.3 = (f32[128,256]{1,0:T(8,128)S(1)}, f32[128,256]{1,0:T(8,128)S(1)}, u32[]{:S(2)}, u32[]{:S(2)}) collective-permute-start(f32[128,256]{1,0:T(8,128)S(1)} %get-tuple-element.70), channel_id=1, source_target_pairs={{1,0},{2,1},{3,2},{4,3},{5,4},{6,5},{7,6},{8,7},{9,8},{10,9},{11,1... | collective-permute-start | bytes 393224 | tf_op jit(solution)/shard_map/ppermute | solution.py:74
  37.9 15.1 %collective-permute-start.2 = (f32[128,256]{1,0:T(8,128)S(1)}, f32[128,256]{1,0:T(8,128)S(1)}, u32[]{:S(2)}, u32[]{:S(2)}) collective-permute-start(f32[128,256]{1,0:T(8,128)S(1)} %get-tuple-element.71), channel_id=1, source_target_pairs={{0,1},{1,2},{2,3},{3,4},{4,5},{5,6},{6,7},{7,8},{8,9},{9,10},{10,1... | collective-permute-start | bytes 393224 | tf_op jit(solution)/shard_map/ppermute | solution.py:73
  53.0 48.1 %copy-start.2 = (f32[2048]{0:T(1024)S(1)}, f32[2048]{0:T(1024)}, u32[]{:S(2)}) copy-start(f32[2048]{0:T(1024)} %param.12) | copy-start | bytes 24580
  56.1 4.5 %collective-permute-start.4 = (f32[160,128]{1,0:T(8,128)S(1)}, f32[160,128]{1,0:T(8,128)S(1)}, u32[]{:S(2)}, u32[]{:S(2)}) collective-permute-start(f32[160,128]{1,0:T(8,128)S(1)} %get-tuple-element.46), channel_id=1, source_target_pairs={{0,16},{1,17},{2,18},{3,19},{4,20},{5,21},{6,22},{7,23},{8,24},{9,... | collective-permute-start | bytes 245768 | tf_op jit(solution)/shard_map/ppermute | solution.py:36
  56.2 6.2 %collective-permute-start.5 = (f32[160,128]{1,0:T(8,128)S(1)}, f32[160,128]{1,0:T(8,128)S(1)}, u32[]{:S(2)}, u32[]{:S(2)}) collective-permute-start(f32[160,128]{1,0:T(8,128)S(1)} %get-tuple-element.47), channel_id=1, source_target_pairs={{0,32},{1,33},{2,34},{3,35},{4,36},{5,37},{6,38},{7,39},{8,40},{9,... | collective-permute-start | bytes 245768 | tf_op jit(solution)/shard_map/ppermute | solution.py:36
  59.1 4.4 %collective-permute-start.6 = (f32[160,128]{1,0:T(8,128)S(1)}, f32[160,128]{1,0:T(8,128)S(1)}, u32[]{:S(2)}, u32[]{:S(2)}) collective-permute-start(f32[160,128]{1,0:T(8,128)S(1)} %get-tuple-element.48), channel_id=1, source_target_pairs={{0,48},{1,49},{2,50},{3,51},{4,52},{5,53},{6,54},{7,55},{8,56},{9,... | collective-permute-start | bytes 245768 | tf_op jit(solution)/shard_map/ppermute | solution.py:36
  63.6 1.4 collective-permute-start.7
  65.0 7.6 %collective-permute-start.10 = (f32[160,128]{1,0:T(8,128)S(1)}, f32[160,128]{1,0:T(8,128)S(1)}, u32[]{:S(2)}, u32[]{:S(2)}) collective-permute-start(f32[160,128]{1,0:T(8,128)S(1)} %add.74), channel_id=1, source_target_pairs={{0,12},{1,13},{2,14},{3,15},{4,8},{5,9},{6,10},{7,11},{8,4},{9,5},... | collective-permute-start | bytes 245768 | tf_op jit(solution)/shard_map/ppermute | solution.py:36
  65.4 7.1 %collective-permute-start.9 = (f32[160,128]{1,0:T(8,128)S(1)}, f32[160,128]{1,0:T(8,128)S(1)}, u32[]{:S(2)}, u32[]{:S(2)}) collective-permute-start(f32[160,128]{1,0:T(8,128)S(1)} %add.74), channel_id=1, source_target_pairs={{0,8},{1,9},{2,10},{3,11},{4,12},{5,13},{6,14},{7,15},{8,0},{9,1},... | collective-permute-start | bytes 245768 | tf_op jit(solution)/shard_map/ppermute | solution.py:36
  66.5 6.5 %collective-permute-start.8 = (f32[160,128]{1,0:T(8,128)S(1)}, f32[160,128]{1,0:T(8,128)S(1)}, u32[]{:S(2)}, u32[]{:S(2)}) collective-permute-start(f32[160,128]{1,0:T(8,128)S(1)} %add.74), channel_id=1, source_target_pairs={{0,4},{1,5},{2,6},{3,7},{4,0},{5,1},{6,2},{7,3},{8,12},{9,13},{10,... | collective-permute-start | bytes 245768 | tf_op jit(solution)/shard_map/ppermute | solution.py:36
  73.1 7.6 %collective-permute-start.13 = (f32[160,128]{1,0:T(8,128)S(1)}, f32[160,128]{1,0:T(8,128)S(1)}, u32[]{:S(2)}, u32[]{:S(2)}) collective-permute-start(f32[160,128]{1,0:T(8,128)S(1)} %add_add_fusion.4), channel_id=1, source_target_pairs={{0,192},{1,193},{2,194},{3,195},{4,196},{5,197},{6,198},{7,199},{8... | collective-permute-start | bytes 245768 | tf_op jit(solution)/shard_map/ppermute | solution.py:36
  77.9 6.2 %collective-permute-start.12 = (f32[160,128]{1,0:T(8,128)S(1)}, f32[160,128]{1,0:T(8,128)S(1)}, u32[]{:S(2)}, u32[]{:S(2)}) collective-permute-start(f32[160,128]{1,0:T(8,128)S(1)} %add_add_fusion.4), channel_id=1, source_target_pairs={{0,128},{1,129},{2,130},{3,131},{4,132},{5,133},{6,134},{7,135},{8... | collective-permute-start | bytes 245768 | tf_op jit(solution)/shard_map/ppermute | solution.py:36
  77.9 6.2 %collective-permute-start.11 = (f32[160,128]{1,0:T(8,128)S(1)}, f32[160,128]{1,0:T(8,128)S(1)}, u32[]{:S(2)}, u32[]{:S(2)}) collective-permute-start(f32[160,128]{1,0:T(8,128)S(1)} %add_add_fusion.4), channel_id=1, source_target_pairs={{0,64},{1,65},{2,66},{3,67},{4,68},{5,69},{6,70},{7,71},{8,72},{9,... | collective-permute-start | bytes 245768 | tf_op jit(solution)/shard_map/ppermute | solution.py:36
  84.2 8.5 %collective-permute-start.14 = (f32[160,128]{1,0:T(8,128)S(1)}, f32[160,128]{1,0:T(8,128)S(1)}, u32[]{:S(2)}, u32[]{:S(2)}) collective-permute-start(f32[160,128]{1,0:T(8,128)S(1)} %add_add_fusion.3), channel_id=1, source_target_pairs={{0,1},{1,0},{2,3},{3,2},{4,5},{5,4},{6,7},{7,6},{8,9},{9,8},{10,11... | collective-permute-start | bytes 245768 | tf_op jit(solution)/shard_map/ppermute | solution.py:36
  92.7 4.9 %collective-permute-start.17 = (f32[160,128]{1,0:T(8,128)S(1)}, f32[160,128]{1,0:T(8,128)S(1)}, u32[]{:S(2)}, u32[]{:S(2)}) collective-permute-start(f32[160,128]{1,0:T(8,128)S(1)} %add.81.refs_1_), channel_id=1, source_target_pairs={{0,48},{1,49},{2,50},{3,51},{4,52},{5,53},{6,54},{7,55},{8,56},{9,... | collective-permute-start | bytes 245768 | tf_op jit(solution)/shard_map/ppermute | solution.py:36
  93.0 6.3 %collective-permute-start.16 = (f32[160,128]{1,0:T(8,128)S(1)}, f32[160,128]{1,0:T(8,128)S(1)}, u32[]{:S(2)}, u32[]{:S(2)}) collective-permute-start(f32[160,128]{1,0:T(8,128)S(1)} %add.81.refs_1_), channel_id=1, source_target_pairs={{0,32},{1,33},{2,34},{3,35},{4,36},{5,37},{6,38},{7,39},{8,40},{9,... | collective-permute-start | bytes 245768 | tf_op jit(solution)/shard_map/ppermute | solution.py:36
  96.7 4.4 %collective-permute-start.15 = (f32[160,128]{1,0:T(8,128)S(1)}, f32[160,128]{1,0:T(8,128)S(1)}, u32[]{:S(2)}, u32[]{:S(2)}) collective-permute-start(f32[160,128]{1,0:T(8,128)S(1)} %add.81.refs_1_), channel_id=1, source_target_pairs={{0,16},{1,17},{2,18},{3,19},{4,20},{5,21},{6,22},{7,23},{8,24},{9,... | collective-permute-start | bytes 245768 | tf_op jit(solution)/shard_map/ppermute | solution.py:36
  101.1 25.0 %copy-start = (f32[16,3,128,128]{3,2,1,0:T(8,128)S(1)}, f32[16,3,128,128]{3,2,1,0:T(8,128)}, u32[]{:S(2)}) copy-start(f32[16,3,128,128]{3,2,1,0:T(8,128)} %k_ref.11) | copy-start | bytes 9437188
  116.4 16.7 %collective-permute-start.19 = (f32[64,256]{1,0:T(8,128)S(1)}, f32[64,256]{1,0:T(8,128)S(1)}, u32[]{:S(2)}, u32[]{:S(2)}) collective-permute-start(f32[64,256]{1,0:T(8,128)S(1)} %get-tuple-element.74), channel_id=1, source_target_pairs={{1,0},{2,1},{3,2},{4,3},{5,4},{6,5},{7,6},{8,7},{9,8},{10,9},{11,1... | collective-permute-start | bytes 196616 | tf_op jit(solution)/shard_map/ppermute | solution.py:74
  118.7 14.3 %collective-permute-start.18 = (f32[64,256]{1,0:T(8,128)S(1)}, f32[64,256]{1,0:T(8,128)S(1)}, u32[]{:S(2)}, u32[]{:S(2)}) collective-permute-start(f32[64,256]{1,0:T(8,128)S(1)} %get-tuple-element.75), channel_id=1, source_target_pairs={{0,1},{1,2},{2,3},{3,4},{4,5},{5,6},{6,7},{7,8},{8,9},{9,10},{10,1... | collective-permute-start | bytes 196616 | tf_op jit(solution)/shard_map/ppermute | solution.py:73
  136.2 1.4 collective-permute-start.20
  137.6 6.2 %collective-permute-start.23 = (f32[192,128]{1,0:T(8,128)S(1)}, f32[192,128]{1,0:T(8,128)S(1)}, u32[]{:S(2)}, u32[]{:S(2)}) collective-permute-start(f32[192,128]{1,0:T(8,128)S(1)} %add.82), channel_id=1, source_target_pairs={{0,48},{1,49},{2,50},{3,51},{4,52},{5,53},{6,54},{7,55},{8,56},{9,... | collective-permute-start | bytes 294920 | tf_op jit(solution)/shard_map/ppermute | solution.py:36
  139.7 7.1 %collective-permute-start.22 = (f32[192,128]{1,0:T(8,128)S(1)}, f32[192,128]{1,0:T(8,128)S(1)}, u32[]{:S(2)}, u32[]{:S(2)}) collective-permute-start(f32[192,128]{1,0:T(8,128)S(1)} %add.82), channel_id=1, source_target_pairs={{0,32},{1,33},{2,34},{3,35},{4,36},{5,37},{6,38},{7,39},{8,40},{9,... | collective-permute-start | bytes 294920 | tf_op jit(solution)/shard_map/ppermute | solution.py:36
  141.9 5.0 %collective-permute-start.21 = (f32[192,128]{1,0:T(8,128)S(1)}, f32[192,128]{1,0:T(8,128)S(1)}, u32[]{:S(2)}, u32[]{:S(2)}) collective-permute-start(f32[192,128]{1,0:T(8,128)S(1)} %add.82), channel_id=1, source_target_pairs={{0,16},{1,17},{2,18},{3,19},{4,20},{5,21},{6,22},{7,23},{8,24},{9,... | collective-permute-start | bytes 294920 | tf_op jit(solution)/shard_map/ppermute | solution.py:36
  146.9 7.0 %collective-permute-start.26 = (f32[192,128]{1,0:T(8,128)S(1)}, f32[192,128]{1,0:T(8,128)S(1)}, u32[]{:S(2)}, u32[]{:S(2)}) collective-permute-start(f32[192,128]{1,0:T(8,128)S(1)} %add_add_fusion.2), channel_id=1, source_target_pairs={{0,12},{1,13},{2,14},{3,15},{4,8},{5,9},{6,10},{7,11},{8,4},{9,5},... | collective-permute-start | bytes 294920 | tf_op jit(solution)/shard_map/ppermute | solution.py:36
  148.7 6.4 %collective-permute-start.25 = (f32[192,128]{1,0:T(8,128)S(1)}, f32[192,128]{1,0:T(8,128)S(1)}, u32[]{:S(2)}, u32[]{:S(2)}) collective-permute-start(f32[192,128]{1,0:T(8,128)S(1)} %add_add_fusion.2), channel_id=1, source_target_pairs={{0,8},{1,9},{2,10},{3,11},{4,12},{5,13},{6,14},{7,15},{8,0},{9,1},... | collective-permute-start | bytes 294920 | tf_op jit(solution)/shard_map/ppermute | solution.py:36
  149.4 5.7 %collective-permute-start.24 = (f32[192,128]{1,0:T(8,128)S(1)}, f32[192,128]{1,0:T(8,128)S(1)}, u32[]{:S(2)}, u32[]{:S(2)}) collective-permute-start(f32[192,128]{1,0:T(8,128)S(1)} %add_add_fusion.2), channel_id=1, source_target_pairs={{0,4},{1,5},{2,6},{3,7},{4,0},{5,1},{6,2},{7,3},{8,12},{9,13},{10,... | collective-permute-start | bytes 294920 | tf_op jit(solution)/shard_map/ppermute | solution.py:36
  155.1 7.5 %collective-permute-start.29 = (f32[192,128]{1,0:T(8,128)S(1)}, f32[192,128]{1,0:T(8,128)S(1)}, u32[]{:S(2)}, u32[]{:S(2)}) collective-permute-start(f32[192,128]{1,0:T(8,128)S(1)} %add_add_fusion.1), channel_id=1, source_target_pairs={{0,192},{1,193},{2,194},{3,195},{4,196},{5,197},{6,198},{7,199},{8... | collective-permute-start | bytes 294920 | tf_op jit(solution)/shard_map/ppermute | solution.py:36
  157.1 8.0 %collective-permute-start.28 = (f32[192,128]{1,0:T(8,128)S(1)}, f32[192,128]{1,0:T(8,128)S(1)}, u32[]{:S(2)}, u32[]{:S(2)}) collective-permute-start(f32[192,128]{1,0:T(8,128)S(1)} %add_add_fusion.1), channel_id=1, source_target_pairs={{0,128},{1,129},{2,130},{3,131},{4,132},{5,133},{6,134},{7,135},{8... | collective-permute-start | bytes 294920 | tf_op jit(solution)/shard_map/ppermute | solution.py:36
  157.7 7.4 %collective-permute-start.27 = (f32[192,128]{1,0:T(8,128)S(1)}, f32[192,128]{1,0:T(8,128)S(1)}, u32[]{:S(2)}, u32[]{:S(2)}) collective-permute-start(f32[192,128]{1,0:T(8,128)S(1)} %add_add_fusion.1), channel_id=1, source_target_pairs={{0,64},{1,65},{2,66},{3,67},{4,68},{5,69},{6,70},{7,71},{8,72},{9,... | collective-permute-start | bytes 294920 | tf_op jit(solution)/shard_map/ppermute | solution.py:36
  165.1 9.3 %collective-permute-start.30 = (f32[192,128]{1,0:T(8,128)S(1)}, f32[192,128]{1,0:T(8,128)S(1)}, u32[]{:S(2)}, u32[]{:S(2)}) collective-permute-start(f32[192,128]{1,0:T(8,128)S(1)} %add_add_fusion), channel_id=1, source_target_pairs={{0,1},{1,0},{2,3},{3,2},{4,5},{5,4},{6,7},{7,6},{8,9},{9,8},{10,11... | collective-permute-start | bytes 294920 | tf_op jit(solution)/shard_map/ppermute | solution.py:36
